TPU v7x, 128 devices: a whole 4x4x4 slice. The times are simulated.
128 devices in a mesh: gx: 8 (over y, core), gy: 16 (over z, x).
Axes of the slice: x: 4, y: 4, z: 4, core: 2. Of those that a mesh axis runs over, the one named last changes fastest.
Arguments:
- ice_volume: float32 [5, 2048, 4096], P(None, 'gy', 'gx'), may hold values from 0.1 to 1
- ice_area: float32 [5, 2048, 4096], P(None, 'gy', 'gx'), may hold values from 0.15 to 0.2
- velocity: float32 [2, 2048, 4096], P(None, 'gy', 'gx'), may hold values from -3 to 3
- forcing: float32 [2, 2048, 4096], P(None, 'gy', 'gx'), may hold values from -6 to 6
- current: float32 [2, 2048, 4096], P(None, 'gy', 'gx'), may hold values from -3 to 3
- stress: float32 [3, 2048, 4096], P(None, 'gy', 'gx'), may hold values from -3 to 3
- ice_mask: int32 [2048, 4096], P('gy', 'gx'), may hold values from 0 to 1
- block_owner: int32 [128, 256], P('gy', 'gx'), may hold values from -1 to 15, as said below
Outputs:
- stress_out: float32 [3, 2048, 4096], P(None, 'gy', 'gx')
- ice_velocity: float32 [2, 8, 4096, 256], P(None, 'gx', 'gy')
Inputs may be any that keep to these rules, and one draw needn't show every extreme that they name: `block_owner`: -1 exactly on the blocks with no ice cell; on every other block the gy index of its owner, which lies in the same gx column; one device's tile hands at most 16 blocks to one owner, and in every draw some tiles hand exactly 16 to every owner.
All inputs are finite; a program needn't handle non-finite values.
Results may differ from a plain program's by a relative error of at most 0.00002.
Values sent between devices are 32-bit elements; how exact they have to be, the bound alone decides.
A program may use at most 192 MiB of HBM per device.

v0:
```python
import jax
import jax.numpy as jnp
from jax import lax
from jax.sharding import PartitionSpec as P

BLOCK = 16
SUBCYCLES = 4


STRENGTH_SCALE = 2.0
CONC_DECAY = 20.0
ECC_SQUARED = 4.0
DELTA_FLOOR = 0.1
STRESS_RATE = 0.5
MASS_BASE = 0.5
WATER_DRAG = 0.5
CORIOLIS = 0.3


def from_behind(value, axis, steps):
    count = lax.axis_size(axis)
    initial, last = (max(0, -steps), min(count, count - steps))
    return lax.ppermute(value, axis, [(source, source + steps) for source in range(initial, last)])


def stress_half(
    sig_one, sig_two, sig_shear, strain_lon, strain_lat, strain_cross, strength, icemask
):
    divergence = strain_lon + strain_lat
    tension = strain_lon - strain_lat
    shearing = 2.0 * strain_cross
    delta = jnp.sqrt(
        divergence * divergence
        + (tension * tension + shearing * shearing) / ECC_SQUARED
        + DELTA_FLOOR * DELTA_FLOOR
    )
    ratio = strength / delta
    relax_factor = 1.0 + STRESS_RATE
    new_one = (sig_one + STRESS_RATE * (ratio * divergence - strength)) / relax_factor * icemask
    new_two = (sig_two + STRESS_RATE * ratio * tension / ECC_SQUARED) / relax_factor * icemask
    new_shear = (
        (sig_shear + STRESS_RATE * ratio * shearing / (2.0 * ECC_SQUARED)) / relax_factor * icemask
    )
    return (new_one, new_two, new_shear)


def momentum_half(
    vel_east,
    vel_north,
    normal_east,
    normal_north,
    sig_shear,
    east_behind,
    shear_behind_lon,
    shear_behind_lat,
    north_behind,
    mass,
    drive_east,
    drive_north,
    icemask,
):
    force_east = normal_east - east_behind + (sig_shear - shear_behind_lat)
    force_north = sig_shear - shear_behind_lon + (normal_north - north_behind)
    denominator = mass + WATER_DRAG
    new_east = (
        (mass * vel_east + force_east + drive_east + CORIOLIS * mass * vel_north)
        / denominator
        * icemask
    )
    new_north = (
        (mass * vel_north + force_north + drive_north - CORIOLIS * mass * vel_east)
        / denominator
        * icemask
    )
    return (new_east, new_north)


def to_blocks(tile, block_rows, block_cols):
    channels = tile.shape[0]
    shaped = tile.reshape(channels, block_rows, BLOCK, block_cols, BLOCK).transpose(1, 3, 0, 2, 4)
    return shaped.reshape(block_rows * block_cols, channels, BLOCK * BLOCK)


def per_device(ice_volume, ice_area, velocity, forcing, current, stress, ice_mask, block_owner):
    icemask = ice_mask.astype(jnp.float32)
    total_volume = jnp.sum(ice_volume, axis=0)
    concentration = jnp.sum(ice_area, axis=0)
    strength = STRENGTH_SCALE * total_volume * jnp.exp(-CONC_DECAY * (1.0 - concentration))
    mass = MASS_BASE + total_volume
    drive_east = forcing[0] + WATER_DRAG * current[0]
    drive_north = forcing[1] + WATER_DRAG * current[1]
    vel_east = velocity[0] * icemask
    vel_north = velocity[1] * icemask
    sig_one = stress[0] * icemask
    sig_two = stress[1] * icemask
    sig_shear = stress[2] * icemask
    block_rows = block_owner.shape[0]
    block_cols = block_owner.shape[1]
    slot_total = block_rows * block_cols
    owner_count = lax.axis_size("gy")
    capacity = slot_total // owner_count
    owners = block_owner.reshape(slot_total)
    is_iced = owners >= 0
    onehot = (owners[:, None] == jnp.arange(owner_count, dtype=jnp.int32)[None, :]).astype(
        jnp.int32
    )
    ranks = jnp.sum(onehot * (jnp.cumsum(onehot, axis=0) - 1), axis=1)
    slot_of = jnp.where(is_iced, owners * capacity + ranks, 0)
    slot_range = jnp.arange(slot_total, dtype=jnp.int32)
    chooser = (slot_of[None, :] == slot_range[:, None]) & is_iced[None, :]
    source_block = jnp.sum(chooser.astype(jnp.int32) * slot_range[None, :], axis=1)
    slot_live = jnp.any(chooser, axis=1).astype(jnp.float32)
    for number in range(SUBCYCLES):
        both_vel = jnp.stack([vel_east, vel_north])
        east_column = from_behind(both_vel[:, :, 0:1], "gx", -1)
        north_row = from_behind(both_vel[:, 0:1, :], "gy", -1)
        ahead_lon = jnp.concatenate([both_vel[:, :, 1:], east_column], axis=2)
        ahead_lat = jnp.concatenate([both_vel[:, 1:, :], north_row], axis=1)
        strain_lon = ahead_lon[0] - vel_east
        strain_lat = ahead_lat[1] - vel_north
        strain_cross = 0.5 * (ahead_lat[0] - vel_east + (ahead_lon[1] - vel_north))
        sig_one, sig_two, sig_shear = stress_half(
            sig_one, sig_two, sig_shear, strain_lon, strain_lat, strain_cross, strength, icemask
        )
        normal_east = 0.5 * (sig_one + sig_two)
        normal_north = 0.5 * (sig_one - sig_two)
        stacked = jnp.stack([normal_east, normal_north, sig_shear])
        west_column = from_behind(stacked[:, :, -1:], "gx", 1)
        south_row = from_behind(stacked[:, -1:, :], "gy", 1)
        behind_lon = jnp.concatenate([west_column, stacked[:, :, :-1]], axis=2)
        behind_lat = jnp.concatenate([south_row, stacked[:, :-1, :]], axis=1)
        vel_east, vel_north = momentum_half(
            vel_east,
            vel_north,
            normal_east,
            normal_north,
            sig_shear,
            behind_lon[0],
            behind_lon[2],
            behind_lat[2],
            behind_lat[1],
            mass,
            drive_east,
            drive_north,
            icemask,
        )
    stress_out = jnp.stack([sig_one, sig_two, sig_shear])
    vel_blocks = to_blocks(jnp.stack([vel_east, vel_north]), block_rows, block_cols)
    outgoing_vel = jnp.take(vel_blocks, source_block, axis=0) * slot_live[:, None, None]
    outgoing_vel = outgoing_vel.reshape(owner_count, capacity, 2, BLOCK * BLOCK)
    arrived = lax.all_to_all(outgoing_vel, "gy", split_axis=0, concat_axis=0, tiled=True)
    ice_velocity = arrived.reshape(slot_total, 2, BLOCK * BLOCK).transpose(1, 0, 2)[:, None]
    return (stress_out, ice_velocity)


def solution(mesh):
    in_specs = (
        P(None, "gy", "gx"),
        P(None, "gy", "gx"),
        P(None, "gy", "gx"),
        P(None, "gy", "gx"),
        P(None, "gy", "gx"),
        P(None, "gy", "gx"),
        P("gy", "gx"),
        P("gy", "gx"),
    )
    out_specs = (P(None, "gy", "gx"), P(None, "gx", "gy", None))
    return jax.shard_map(
        per_device, mesh=mesh, in_specs=in_specs, out_specs=out_specs, check_vma=False
    )
```

profile of v0, /device:TPU:1, one launch (start us, length us, event | category | flops | bytes accessed | tf_op | source)
XLA Modules:
  0.0 126.9 jit_solution(17597453985809539052)
XLA Ops:
  2.4 1.3 %collective-permute-start.1 = (f32[2,1,512]{2,1,0:T(1,128)}, f32[2,1,512]{2,1,0:T(1,128)}, u32[]{:S(2)}, u32[]{:S(2)}) collective-permute-start(f32[2,1,512]{2,1,0:T(1,128)} %pad_maximum_fusion.27), channel_id=1, source_target_pairs={{1,0},{2,1},{3,2},{4,3},{5,4},{6,5},{7,6},{8,7},{9,8},{10,9},{11,1... | collective-permute-start | bytes 12296 | tf_op jit(solution)/shard_map/ppermute | solution.py:23
  4.4 3.3 %collective-permute-start = (f32[2,128,1]{2,1,0:T(8,128)}, f32[2,128,1]{2,1,0:T(8,128)S(1)}, u32[]{:S(2)}, u32[]{:S(2)}) collective-permute-start(f32[2,128,1]{2,1,0:T(8,128)} %fusion.138), channel_id=1, source_target_pairs={{16,0},{32,16},{48,32},{64,48},{80,64},{96,80},{112,96},{17,1},{33... | collective-permute-start | bytes 3080 | tf_op jit(solution)/shard_map/ppermute | solution.py:23
  9.6 1.5 %reduce_sum.41 = f32[128,512]{1,0:T(8,128)S(1)} reduce(f32[5,128,512]{2,1,0:T(8,128)} %param.9, f32[]{:T(128)} %constant.62.clone.1), dimensions={0}, to_apply=%region_1.0 | reduce | flops 262144 | bytes 1572868 | tf_op jit(solution)/shard_map/reduce_sum | solution.py:87
  11.1 1.5 %reduce_sum.40 = f32[128,512]{1,0:T(8,128)S(1)} reduce(f32[5,128,512]{2,1,0:T(8,128)} %param.8, f32[]{:T(128)} %constant.62.clone.1), dimensions={0}, to_apply=%region_0.0 | reduce | flops 262144 | bytes 1572868 | tf_op jit(solution)/shard_map/reduce_sum | solution.py:86
  14.2 4.3 %collective-permute-start.3 = (f32[3,1,512]{2,1,0:T(1,128)S(1)}, f32[3,1,512]{2,1,0:T(1,128)S(1)}, u32[]{:S(2)}, u32[]{:S(2)}) collective-permute-start(f32[3,1,512]{2,1,0:T(1,128)S(1)} %pad_maximum_fusion.23), channel_id=1, source_target_pairs={{0,1},{1,2},{2,3},{3,4},{4,5},{5,6},{6,7},{7,8},{8,9},{9,10},{10,1... | collective-permute-start | bytes 18440 | tf_op jit(solution)/shard_map/ppermute | solution.py:23
  18.6 3.5 %collective-permute-start.2 = (f32[3,128,1]{2,1,0:T(8,128)S(1)}, f32[3,128,1]{2,1,0:T(8,128)S(1)}, u32[]{:S(2)}, u32[]{:S(2)}) collective-permute-start(f32[3,128,1]{2,1,0:T(8,128)S(1)} %slice.312), channel_id=1, source_target_pairs={{0,16},{16,32},{32,48},{48,64},{64,80},{80,96},{96,112},{1,17},{17... | collective-permute-start | bytes 4616 | tf_op jit(solution)/shard_map/ppermute | solution.py:23
  22.0 2.6 %collective-permute-done.2 = f32[3,128,1]{2,1,0:T(8,128)S(1)} collective-permute-done((f32[3,128,1]{2,1,0:T(8,128)S(1)}, f32[3,128,1]{2,1,0:T(8,128)S(1)}, u32[]{:S(2)}, u32[]{:S(2)}) %collective-permute-start.2) | collective-permute-done | bytes 1568 | tf_op jit(solution)/shard_map/ppermute | solution.py:23
  25.5 1.3 %collective-permute-start.5 = (f32[2,1,512]{2,1,0:T(1,128)S(1)}, f32[2,1,512]{2,1,0:T(1,128)S(1)}, u32[]{:S(2)}, u32[]{:S(2)}) collective-permute-start(f32[2,1,512]{2,1,0:T(1,128)S(1)} %pad_maximum_fusion.26), channel_id=1, source_target_pairs={{1,0},{2,1},{3,2},{4,3},{5,4},{6,5},{7,6},{8,7},{9,8},{10,9},{11,1... | collective-permute-start | bytes 12296 | tf_op jit(solution)/shard_map/ppermute | solution.py:23
  26.8 1.9 %collective-permute-start.4 = (f32[2,128,1]{2,1,0:T(8,128)S(1)}, f32[2,128,1]{2,1,0:T(8,128)S(1)}, u32[]{:S(2)}, u32[]{:S(2)}) collective-permute-start(f32[2,128,1]{2,1,0:T(8,128)S(1)} %fusion.137), channel_id=1, source_target_pairs={{16,0},{32,16},{48,32},{64,48},{80,64},{96,80},{112,96},{17,1},{33... | collective-permute-start | bytes 3080 | tf_op jit(solution)/shard_map/ppermute | solution.py:23
  28.9 4.9 %collective-permute-done.4 = f32[2,128,1]{2,1,0:T(8,128)S(1)} collective-permute-done((f32[2,128,1]{2,1,0:T(8,128)S(1)}, f32[2,128,1]{2,1,0:T(8,128)S(1)}, u32[]{:S(2)}, u32[]{:S(2)}) %collective-permute-start.4) | collective-permute-done | bytes 1056 | tf_op jit(solution)/shard_map/ppermute | solution.py:23
  34.5 4.3 %collective-permute-start.7 = (f32[3,1,512]{2,1,0:T(1,128)S(1)}, f32[3,1,512]{2,1,0:T(1,128)S(1)}, u32[]{:S(2)}, u32[]{:S(2)}) collective-permute-start(f32[3,1,512]{2,1,0:T(1,128)S(1)} %pad_maximum_fusion.22), channel_id=1, source_target_pairs={{0,1},{1,2},{2,3},{3,4},{4,5},{5,6},{6,7},{7,8},{8,9},{9,10},{10,1... | collective-permute-start | bytes 18440 | tf_op jit(solution)/shard_map/ppermute | solution.py:23
  38.9 2.1 %collective-permute-start.6 = (f32[3,128,1]{2,1,0:T(8,128)S(1)}, f32[3,128,1]{2,1,0:T(8,128)S(1)}, u32[]{:S(2)}, u32[]{:S(2)}) collective-permute-start(f32[3,128,1]{2,1,0:T(8,128)S(1)} %slice.325), channel_id=1, source_target_pairs={{0,16},{16,32},{32,48},{48,64},{64,80},{80,96},{96,112},{1,17},{17... | collective-permute-start | bytes 4616 | tf_op jit(solution)/shard_map/ppermute | solution.py:23
  41.0 2.6 %collective-permute-done.6 = f32[3,128,1]{2,1,0:T(8,128)S(1)} collective-permute-done((f32[3,128,1]{2,1,0:T(8,128)S(1)}, f32[3,128,1]{2,1,0:T(8,128)S(1)}, u32[]{:S(2)}, u32[]{:S(2)}) %collective-permute-start.6) | collective-permute-done | bytes 1568 | tf_op jit(solution)/shard_map/ppermute | solution.py:23
  44.2 1.3 %collective-permute-start.9 = (f32[2,1,512]{2,1,0:T(1,128)S(1)}, f32[2,1,512]{2,1,0:T(1,128)S(1)}, u32[]{:S(2)}, u32[]{:S(2)}) collective-permute-start(f32[2,1,512]{2,1,0:T(1,128)S(1)} %pad_maximum_fusion.25), channel_id=1, source_target_pairs={{1,0},{2,1},{3,2},{4,3},{5,4},{6,5},{7,6},{8,7},{9,8},{10,9},{11,1... | collective-permute-start | bytes 12296 | tf_op jit(solution)/shard_map/ppermute | solution.py:23
  45.5 1.9 %collective-permute-start.8 = (f32[2,128,1]{2,1,0:T(8,128)S(1)}, f32[2,128,1]{2,1,0:T(8,128)S(1)}, u32[]{:S(2)}, u32[]{:S(2)}) collective-permute-start(f32[2,128,1]{2,1,0:T(8,128)S(1)} %fusion.136), channel_id=1, source_target_pairs={{16,0},{32,16},{48,32},{64,48},{80,64},{96,80},{112,96},{17,1},{33... | collective-permute-start | bytes 3080 | tf_op jit(solution)/shard_map/ppermute | solution.py:23
  47.6 4.9 %collective-permute-done.8 = f32[2,128,1]{2,1,0:T(8,128)S(1)} collective-permute-done((f32[2,128,1]{2,1,0:T(8,128)S(1)}, f32[2,128,1]{2,1,0:T(8,128)S(1)}, u32[]{:S(2)}, u32[]{:S(2)}) %collective-permute-start.8) | collective-permute-done | bytes 1056 | tf_op jit(solution)/shard_map/ppermute | solution.py:23
  53.2 4.3 %collective-permute-start.11 = (f32[3,1,512]{2,1,0:T(1,128)S(1)}, f32[3,1,512]{2,1,0:T(1,128)S(1)}, u32[]{:S(2)}, u32[]{:S(2)}) collective-permute-start(f32[3,1,512]{2,1,0:T(1,128)S(1)} %pad_maximum_fusion.21), channel_id=1, source_target_pairs={{0,1},{1,2},{2,3},{3,4},{4,5},{5,6},{6,7},{7,8},{8,9},{9,10},{10,1... | collective-permute-start | bytes 18440 | tf_op jit(solution)/shard_map/ppermute | solution.py:23
  57.6 2.7 %collective-permute-start.10 = (f32[3,128,1]{2,1,0:T(8,128)S(1)}, f32[3,128,1]{2,1,0:T(8,128)S(1)}, u32[]{:S(2)}, u32[]{:S(2)}) collective-permute-start(f32[3,128,1]{2,1,0:T(8,128)S(1)} %slice.338), channel_id=1, source_target_pairs={{0,16},{16,32},{32,48},{48,64},{64,80},{80,96},{96,112},{1,17},{17... | collective-permute-start | bytes 4616 | tf_op jit(solution)/shard_map/ppermute | solution.py:23
  60.5 2.5 %collective-permute-done.10 = f32[3,128,1]{2,1,0:T(8,128)S(1)} collective-permute-done((f32[3,128,1]{2,1,0:T(8,128)S(1)}, f32[3,128,1]{2,1,0:T(8,128)S(1)}, u32[]{:S(2)}, u32[]{:S(2)}) %collective-permute-start.10) | collective-permute-done | bytes 1568 | tf_op jit(solution)/shard_map/ppermute | solution.py:23
  63.5 1.3 %collective-permute-start.13 = (f32[2,1,512]{2,1,0:T(1,128)S(1)}, f32[2,1,512]{2,1,0:T(1,128)S(1)}, u32[]{:S(2)}, u32[]{:S(2)}) collective-permute-start(f32[2,1,512]{2,1,0:T(1,128)S(1)} %pad_maximum_fusion.24), channel_id=1, source_target_pairs={{1,0},{2,1},{3,2},{4,3},{5,4},{6,5},{7,6},{8,7},{9,8},{10,9},{11,1... | collective-permute-start | bytes 12296 | tf_op jit(solution)/shard_map/ppermute | solution.py:23
  64.8 1.9 %collective-permute-start.12 = (f32[2,128,1]{2,1,0:T(8,128)S(1)}, f32[2,128,1]{2,1,0:T(8,128)S(1)}, u32[]{:S(2)}, u32[]{:S(2)}) collective-permute-start(f32[2,128,1]{2,1,0:T(8,128)S(1)} %fusion.135), channel_id=1, source_target_pairs={{16,0},{32,16},{48,32},{64,48},{80,64},{96,80},{112,96},{17,1},{33... | collective-permute-start | bytes 3080 | tf_op jit(solution)/shard_map/ppermute | solution.py:23
  66.9 4.9 %collective-permute-done.12 = f32[2,128,1]{2,1,0:T(8,128)S(1)} collective-permute-done((f32[2,128,1]{2,1,0:T(8,128)S(1)}, f32[2,128,1]{2,1,0:T(8,128)S(1)}, u32[]{:S(2)}, u32[]{:S(2)}) %collective-permute-start.12) | collective-permute-done | bytes 1056 | tf_op jit(solution)/shard_map/ppermute | solution.py:23
  74.3 5.1 %collective-permute-start.15 = (f32[3,1,512]{2,1,0:T(1,128)S(1)}, f32[3,1,512]{2,1,0:T(1,128)S(1)}, u32[]{:S(2)}, u32[]{:S(2)}) collective-permute-start(f32[3,1,512]{2,1,0:T(1,128)S(1)} %slice.354), channel_id=1, source_target_pairs={{0,1},{1,2},{2,3},{3,4},{4,5},{5,6},{6,7},{7,8},{8,9},{9,10},{10,1... | collective-permute-start | bytes 18440 | tf_op jit(solution)/shard_map/ppermute | solution.py:23
  79.5 3.5 %collective-permute-start.14 = (f32[3,128,1]{2,1,0:T(8,128)}, f32[3,128,1]{2,1,0:T(8,128)S(1)}, u32[]{:S(2)}, u32[]{:S(2)}) collective-permute-start(f32[3,128,1]{2,1,0:T(8,128)} %slice.352), channel_id=1, source_target_pairs={{0,16},{16,32},{32,48},{48,64},{64,80},{80,96},{96,112},{1,17},{17... | collective-permute-start | bytes 4616 | tf_op jit(solution)/shard_map/ppermute | solution.py:23
  83.1 2.6 %collective-permute-done.14 = f32[3,128,1]{2,1,0:T(8,128)S(1)} collective-permute-done((f32[3,128,1]{2,1,0:T(8,128)}, f32[3,128,1]{2,1,0:T(8,128)S(1)}, u32[]{:S(2)}, u32[]{:S(2)}) %collective-permute-start.14) | collective-permute-done | bytes 1568 | tf_op jit(solution)/shard_map/ppermute | solution.py:23
  86.4 2.0 %fusion.48 = (f32[128,512]{1,0:T(8,128)S(1)}, f32[128,512]{1,0:T(8,128)}) fusion(f32[128,512]{1,0:T(8,128)S(1)} %multiply_multiply_fusion, f32[3,127,512]{2,1,0:T(8,128)S(1)} %bitcast.435, f32[3,1,512]{2,1,0:T(1,128)S(1)} %collective-permute-done.15, f32[3,128,511]{2,1,0:T(8,128)S(1)} %bitcast.436, f32[3,128,1]{2,1,0:T(8,128)} %copy-done.5, ...), kind=kLoop, calls=%fused_computation.99 | loop fusion | flops 2097152 | bytes 4456448 | tf_op jit(solution)/shard_map/mul | solution.py:66
  88.4 1.7 %stack.135 = f32[1,8,16,32,16]{4,3,2,1,0:T(8,128)S(1)} reshape(f32[128,512]{1,0:T(8,128)} %get-tuple-element.32) | data formatting | bytes 524288 | tf_op jit(solution)/shard_map/stack | solution.py:148
  90.1 2.0 %stack.134 = f32[1,8,16,32,16]{4,3,2,1,0:T(8,128)} reshape(f32[128,512]{1,0:T(8,128)S(1)} %get-tuple-element.31) | data formatting | bytes 524288 | tf_op jit(solution)/shard_map/stack | solution.py:148
  92.2 4.2 %maximum_bitcast_fusion = f32[8,32,2,16,16]{4,1,3,0,2:T(8,128)} fusion(f32[1,8,16,32,16]{4,3,2,1,0:T(8,128)S(1)} %stack.135, f32[1,8,16,32,16]{4,3,2,1,0:T(8,128)} %stack.134), kind=kLoop, calls=%fused_computation.1 | loop fusion | flops 131072 | bytes 1048576 | tf_op jit(solution)/shard_map/transpose | solution.py:80
  96.4 2.9 %copy.15 = f32[8,32,2,16,16]{1,0,4,3,2:T(8,128)S(1)} copy(f32[8,32,2,16,16]{4,1,3,0,2:T(8,128)} %maximum_bitcast_fusion) | data formatting | bytes 1048576 | tf_op jit(solution)/shard_map/transpose | solution.py:80
  100.1 1.2 gather_fusion
  102.1 23.9 %all_to_all.5 = f32[16,16,2,256]{3,2,1,0:T(2,128)S(1)} all-to-all(f32[16,16,2,256]{3,2,1,0:T(2,128)S(1)} %select_multiply_fusion), channel_id=1, replica_groups=mesh['gx'=8,'gy'=16] {'gy'}, dimensions={0} | all-to-all | bytes 1048576 | tf_op jit(solution)/shard_map/all_to_all | solution.py:151
  (94 shorter events, 15.8 us)
Async XLA Ops:
  0.6 7.4 %copy-start.6 = (s32[8,32]{1,0:T(8,128)S(1)}, s32[8,32]{1,0:T(8,128)}, u32[]{:S(2)}) copy-start(s32[8,32]{1,0:T(8,128)} %param.15) | copy-start | bytes 3076
  2.4 10.2 %collective-permute-start.1 = (f32[2,1,512]{2,1,0:T(1,128)}, f32[2,1,512]{2,1,0:T(1,128)}, u32[]{:S(2)}, u32[]{:S(2)}) collective-permute-start(f32[2,1,512]{2,1,0:T(1,128)} %pad_maximum_fusion.27), channel_id=1, source_target_pairs={{1,0},{2,1},{3,2},{4,3},{5,4},{6,5},{7,6},{8,7},{9,8},{10,9},{11,1... | collective-permute-start | bytes 12296 | tf_op jit(solution)/shard_map/ppermute | solution.py:23
  4.4 8.3 %collective-permute-start = (f32[2,128,1]{2,1,0:T(8,128)}, f32[2,128,1]{2,1,0:T(8,128)S(1)}, u32[]{:S(2)}, u32[]{:S(2)}) collective-permute-start(f32[2,128,1]{2,1,0:T(8,128)} %fusion.138), channel_id=1, source_target_pairs={{16,0},{32,16},{48,32},{64,48},{80,64},{96,80},{112,96},{17,1},{33... | collective-permute-start | bytes 3080 | tf_op jit(solution)/shard_map/ppermute | solution.py:23
  7.8 4.9 %copy-start = (s32[128,512]{1,0:T(8,128)S(1)}, s32[128,512]{1,0:T(8,128)}, u32[]{:S(2)}) copy-start(s32[128,512]{1,0:T(8,128)} %param.14) | copy-start | bytes 786436
  7.8 4.9 %copy-start.1 = (f32[2,128,512]{2,1,0:T(8,128)S(1)}, f32[2,128,512]{2,1,0:T(8,128)}, u32[]{:S(2)}) copy-start(f32[2,128,512]{2,1,0:T(8,128)} %param.10) | copy-start | bytes 1572868
  7.8 4.9 %copy-start.2 = (f32[3,128,512]{2,1,0:T(8,128)S(1)}, f32[3,128,512]{2,1,0:T(8,128)}, u32[]{:S(2)}) copy-start(f32[3,128,512]{2,1,0:T(8,128)} %param.13) | copy-start | bytes 2359300
  9.0 0.5 copy-start.7
  13.8 10.8 %copy-start.3 = (f32[2,128,512]{2,1,0:T(8,128)S(1)}, f32[2,128,512]{2,1,0:T(8,128)}, u32[]{:S(2)}) copy-start(f32[2,128,512]{2,1,0:T(8,128)} %param.12) | copy-start | bytes 1572868
  13.9 10.8 %copy-start.4 = (f32[2,128,512]{2,1,0:T(8,128)S(1)}, f32[2,128,512]{2,1,0:T(8,128)}, u32[]{:S(2)}) copy-start(f32[2,128,512]{2,1,0:T(8,128)} %param.11) | copy-start | bytes 1572868
  14.2 10.5 %collective-permute-start.3 = (f32[3,1,512]{2,1,0:T(1,128)S(1)}, f32[3,1,512]{2,1,0:T(1,128)S(1)}, u32[]{:S(2)}, u32[]{:S(2)}) collective-permute-start(f32[3,1,512]{2,1,0:T(1,128)S(1)} %pad_maximum_fusion.23), channel_id=1, source_target_pairs={{0,1},{1,2},{2,3},{3,4},{4,5},{5,6},{6,7},{7,8},{8,9},{9,10},{10,1... | collective-permute-start | bytes 18440 | tf_op jit(solution)/shard_map/ppermute | solution.py:23
  18.6 6.1 %collective-permute-start.2 = (f32[3,128,1]{2,1,0:T(8,128)S(1)}, f32[3,128,1]{2,1,0:T(8,128)S(1)}, u32[]{:S(2)}, u32[]{:S(2)}) collective-permute-start(f32[3,128,1]{2,1,0:T(8,128)S(1)} %slice.312), channel_id=1, source_target_pairs={{0,16},{16,32},{32,48},{48,64},{64,80},{80,96},{96,112},{1,17},{17... | collective-permute-start | bytes 4616 | tf_op jit(solution)/shard_map/ppermute | solution.py:23
  25.5 8.3 %collective-permute-start.5 = (f32[2,1,512]{2,1,0:T(1,128)S(1)}, f32[2,1,512]{2,1,0:T(1,128)S(1)}, u32[]{:S(2)}, u32[]{:S(2)}) collective-permute-start(f32[2,1,512]{2,1,0:T(1,128)S(1)} %pad_maximum_fusion.26), channel_id=1, source_target_pairs={{1,0},{2,1},{3,2},{4,3},{5,4},{6,5},{7,6},{8,7},{9,8},{10,9},{11,1... | collective-permute-start | bytes 12296 | tf_op jit(solution)/shard_map/ppermute | solution.py:23
  26.8 7.0 %collective-permute-start.4 = (f32[2,128,1]{2,1,0:T(8,128)S(1)}, f32[2,128,1]{2,1,0:T(8,128)S(1)}, u32[]{:S(2)}, u32[]{:S(2)}) collective-permute-start(f32[2,128,1]{2,1,0:T(8,128)S(1)} %fusion.137), channel_id=1, source_target_pairs={{16,0},{32,16},{48,32},{64,48},{80,64},{96,80},{112,96},{17,1},{33... | collective-permute-start | bytes 3080 | tf_op jit(solution)/shard_map/ppermute | solution.py:23
  34.5 9.1 %collective-permute-start.7 = (f32[3,1,512]{2,1,0:T(1,128)S(1)}, f32[3,1,512]{2,1,0:T(1,128)S(1)}, u32[]{:S(2)}, u32[]{:S(2)}) collective-permute-start(f32[3,1,512]{2,1,0:T(1,128)S(1)} %pad_maximum_fusion.22), channel_id=1, source_target_pairs={{0,1},{1,2},{2,3},{3,4},{4,5},{5,6},{6,7},{7,8},{8,9},{9,10},{10,1... | collective-permute-start | bytes 18440 | tf_op jit(solution)/shard_map/ppermute | solution.py:23
  38.9 4.7 %collective-permute-start.6 = (f32[3,128,1]{2,1,0:T(8,128)S(1)}, f32[3,128,1]{2,1,0:T(8,128)S(1)}, u32[]{:S(2)}, u32[]{:S(2)}) collective-permute-start(f32[3,128,1]{2,1,0:T(8,128)S(1)} %slice.325), channel_id=1, source_target_pairs={{0,16},{16,32},{32,48},{48,64},{64,80},{80,96},{96,112},{1,17},{17... | collective-permute-start | bytes 4616 | tf_op jit(solution)/shard_map/ppermute | solution.py:23
  44.2 8.3 %collective-permute-start.9 = (f32[2,1,512]{2,1,0:T(1,128)S(1)}, f32[2,1,512]{2,1,0:T(1,128)S(1)}, u32[]{:S(2)}, u32[]{:S(2)}) collective-permute-start(f32[2,1,512]{2,1,0:T(1,128)S(1)} %pad_maximum_fusion.25), channel_id=1, source_target_pairs={{1,0},{2,1},{3,2},{4,3},{5,4},{6,5},{7,6},{8,7},{9,8},{10,9},{11,1... | collective-permute-start | bytes 12296 | tf_op jit(solution)/shard_map/ppermute | solution.py:23
  45.5 7.0 %collective-permute-start.8 = (f32[2,128,1]{2,1,0:T(8,128)S(1)}, f32[2,128,1]{2,1,0:T(8,128)S(1)}, u32[]{:S(2)}, u32[]{:S(2)}) collective-permute-start(f32[2,128,1]{2,1,0:T(8,128)S(1)} %fusion.136), channel_id=1, source_target_pairs={{16,0},{32,16},{48,32},{64,48},{80,64},{96,80},{112,96},{17,1},{33... | collective-permute-start | bytes 3080 | tf_op jit(solution)/shard_map/ppermute | solution.py:23
  52.9 7.4 %copy-start.8 = (pred[256]{0:T(512)(128)(4,1)S(1)}, pred[256]{0:T(512)(128)(4,1)}, u32[]{:S(2)}) copy-start(pred[256]{0:T(512)(128)(4,1)} %copy-done.7) | copy-start | bytes 772
  53.2 9.7 %collective-permute-start.11 = (f32[3,1,512]{2,1,0:T(1,128)S(1)}, f32[3,1,512]{2,1,0:T(1,128)S(1)}, u32[]{:S(2)}, u32[]{:S(2)}) collective-permute-start(f32[3,1,512]{2,1,0:T(1,128)S(1)} %pad_maximum_fusion.21), channel_id=1, source_target_pairs={{0,1},{1,2},{2,3},{3,4},{4,5},{5,6},{6,7},{7,8},{8,9},{9,10},{10,1... | collective-permute-start | bytes 18440 | tf_op jit(solution)/shard_map/ppermute | solution.py:23
  57.6 5.3 %collective-permute-start.10 = (f32[3,128,1]{2,1,0:T(8,128)S(1)}, f32[3,128,1]{2,1,0:T(8,128)S(1)}, u32[]{:S(2)}, u32[]{:S(2)}) collective-permute-start(f32[3,128,1]{2,1,0:T(8,128)S(1)} %slice.338), channel_id=1, source_target_pairs={{0,16},{16,32},{32,48},{48,64},{64,80},{80,96},{96,112},{1,17},{17... | collective-permute-start | bytes 4616 | tf_op jit(solution)/shard_map/ppermute | solution.py:23
  63.5 8.3 %collective-permute-start.13 = (f32[2,1,512]{2,1,0:T(1,128)S(1)}, f32[2,1,512]{2,1,0:T(1,128)S(1)}, u32[]{:S(2)}, u32[]{:S(2)}) collective-permute-start(f32[2,1,512]{2,1,0:T(1,128)S(1)} %pad_maximum_fusion.24), channel_id=1, source_target_pairs={{1,0},{2,1},{3,2},{4,3},{5,4},{6,5},{7,6},{8,7},{9,8},{10,9},{11,1... | collective-permute-start | bytes 12296 | tf_op jit(solution)/shard_map/ppermute | solution.py:23
  64.8 7.0 %collective-permute-start.12 = (f32[2,128,1]{2,1,0:T(8,128)S(1)}, f32[2,128,1]{2,1,0:T(8,128)S(1)}, u32[]{:S(2)}, u32[]{:S(2)}) collective-permute-start(f32[2,128,1]{2,1,0:T(8,128)S(1)} %fusion.135), channel_id=1, source_target_pairs={{16,0},{32,16},{48,32},{64,48},{80,64},{96,80},{112,96},{17,1},{33... | collective-permute-start | bytes 3080 | tf_op jit(solution)/shard_map/ppermute | solution.py:23
  74.3 11.4 %collective-permute-start.15 = (f32[3,1,512]{2,1,0:T(1,128)S(1)}, f32[3,1,512]{2,1,0:T(1,128)S(1)}, u32[]{:S(2)}, u32[]{:S(2)}) collective-permute-start(f32[3,1,512]{2,1,0:T(1,128)S(1)} %slice.354), channel_id=1, source_target_pairs={{0,1},{1,2},{2,3},{3,4},{4,5},{5,6},{6,7},{7,8},{8,9},{9,10},{10,1... | collective-permute-start | bytes 18440 | tf_op jit(solution)/shard_map/ppermute | solution.py:23
  79.5 6.2 %collective-permute-start.14 = (f32[3,128,1]{2,1,0:T(8,128)}, f32[3,128,1]{2,1,0:T(8,128)S(1)}, u32[]{:S(2)}, u32[]{:S(2)}) collective-permute-start(f32[3,128,1]{2,1,0:T(8,128)} %slice.352), channel_id=1, source_target_pairs={{0,16},{16,32},{32,48},{48,64},{64,80},{80,96},{96,112},{1,17},{17... | collective-permute-start | bytes 4616 | tf_op jit(solution)/shard_map/ppermute | solution.py:23
  85.7 0.7 copy-start.5
where the time goes:
time: 128 us; the launch traced here: 127 us
  starting transfers between devices  43.9 us (34%)
  waiting for transfers between devices  25 us (20%)
  blocking collectives  23.9 us (19%)
  other arithmetic  20.5 us (16%)
  local copies, waits for them, and re-layouts  12.4 us (10%)
    ppermute x16, starting transfers between devices, from_behind(): lax.ppermute(value, axis, [(source, source + steps) for source in range(i...  43.9 us
    ppermute x16, waiting for transfers between devices, from_behind(): lax.ppermute(value, axis, [(source, source + steps) for source in range(i...  25 us
    all_to_all x1, blocking collectives, per_device(): lax.all_to_all(outgoing_vel, 'gy', split_axis=0, concat_axis=0, tiled=True)  23.9 us
    transpose x1, other arithmetic, to_blocks(): tile.reshape(channels, block_rows, BLOCK, block_cols, BLOCK)  4.24 us
    another operation x2, local copies, waits for them, and re-layouts, per_device(): jnp.stack([vel_east, vel_north])  3.79 us
    another operation x12, other arithmetic, per_device(): stacked = jnp.stack([normal_east, normal_north, sig_shear])  3.67 us
    another operation x17, other arithmetic, per_device(): both_vel = jnp.stack([vel_east, vel_north])  3.52 us
    mul x4, other arithmetic, momentum_half(): (mass * vel_east + force_east + drive_east + CORIOLIS * mass * vel_north)...  3.28 us
  transfers between devices with their start and end apart: 16, of which 7 were waited for; matrix products, arithmetic and copies ran while one was open for 5% of the time, Pallas kernels for 0%

commit v1 on v0

v1 whole, which is shorter than its diff:
```python
import functools

import jax
import jax.numpy as jnp
from jax import lax
from jax.experimental import pallas as pl
from jax.experimental.pallas import tpu as pltpu
from jax.sharding import PartitionSpec as P

MESH = pl.DeviceIdType.MESH
BLOCK = 16
SUBCYCLES = 4
ROWS, COLS = 128, 512
TOP = 16
HIGH = ROWS + 32
KEEP = 2.0 / 3.0
PEERS = (
    (2, 2), (2, 3), (3, 2), (2, 1), (1, 2), (2, 0), (0, 2), (3, 1),
    (1, 3), (3, 3), (1, 1), (3, 0), (0, 3), (1, 0), (0, 1),
)
U, V, N1, N2, SH, S, B, DE, DN = range(9)


def lanes(n=8):
    return lax.broadcasted_iota(jnp.int32, (n, 128), 1)


def sublanes():
    return lax.broadcasted_iota(jnp.int32, (8, 128), 0)


def prepare(raw, F):
    vol, area, vel, forc, cur, strs, mask = raw

    def rows(i, carry):
        src = pl.ds(pl.multiple_of(i * 8, 8), 8)
        dst = pl.ds(pl.multiple_of(i * 8 + TOP, 8), 8)
        for j in range(4):
            col = pl.ds(j * 128, 128)
            m = mask[src, col].astype(jnp.float32)
            v = [vol[c, src, col] for c in range(5)]
            a = [area[c, src, col] for c in range(5)]
            total = ((v[0] + v[1]) + (v[2] + v[3])) + v[4]
            conc = ((a[0] + a[1]) + (a[2] + a[3])) + a[4]
            strength = 2.0 * total * jnp.exp(-20.0 * (1.0 - conc))
            weight = m / (total + 1.0)
            F[S][j, dst, :] = strength * m * (1.0 / 6.0)
            F[B][j, dst, :] = weight
            F[DE][j, dst, :] = weight * (forc[0, src, col] + 0.5 * cur[0, src, col])
            F[DN][j, dst, :] = weight * (forc[1, src, col] + 0.5 * cur[1, src, col])
            F[U][j, dst, :] = vel[0, src, col] * m
            F[V][j, dst, :] = vel[1, src, col] * m
            half = 0.5 * m
            F[N1][j, dst, :] = half * (strs[0, src, col] + strs[1, src, col])
            F[N2][j, dst, :] = half * (strs[0, src, col] - strs[1, src, col])
            F[SH][j, dst, :] = strs[2, src, col] * m
        return carry

    lax.fori_loop(0, ROWS // 8, rows, 0)


def pack_lon(F, W):
    lane = lanes()

    def rows(i, carry):
        src = pl.ds(pl.multiple_of(i * 8 + TOP, 8), 8)
        out = jnp.zeros((8, 128), jnp.float32)
        for f in range(9):
            x = jnp.where(lane < 64, F[f][0, src, :], F[f][3, src, :])
            x = pltpu.roll(x, 8 * f, 1) if f else x
            here = (lane < 8 * f + 4) & (lane >= 8 * f - 4) if f else (lane < 4) | (lane >= 124)
            out = jnp.where(here, x, out)
        W[pl.ds(pl.multiple_of(i * 8, 8), 8), :] = out
        return carry

    lax.fori_loop(0, ROWS // 8, rows, 0)


def pack_lat(F, send_n, send_s):
    low = sublanes() < 4
    for p in range(5):
        f, g = 2 * p, min(2 * p + 1, 8)
        for j in range(4):
            last = pl.ds(TOP + ROWS - 8, 8)
            first = pl.ds(TOP, 8)
            send_n[p, j] = jnp.where(low, pltpu.roll(F[f][j, last, :], 4, 0), F[g][j, last, :])
            send_s[p, j] = jnp.where(low, F[f][j, first, :], pltpu.roll(F[g][j, first, :], 4, 0))


def unpack_lat(F, recv_s, recv_n, has_s, has_n):
    for p in range(5):
        f, g = 2 * p, 2 * p + 1
        for j in range(4):
            x = recv_s[p, j] * has_s
            y = recv_n[p, j] * has_n
            F[f][j, pl.ds(TOP - 8, 8), :] = pltpu.roll(x, 4, 0)
            F[f][j, pl.ds(TOP + ROWS, 8), :] = y
            if g < 9:
                F[g][j, pl.ds(TOP - 8, 8), :] = x
                F[g][j, pl.ds(TOP + ROWS, 8), :] = pltpu.roll(y, 4, 0)


def unpack_lon(F, WE, WW, has_e, has_w, has_s, has_n):
    ahead = lanes() % 8 < 4

    def tile(r, factor):
        src = pl.ds(r, 8)
        x = jnp.where(ahead, WE[src, :] * (has_e * factor), WW[src, :] * (has_w * factor))
        for f in range(9):
            F[f][4, src, :] = pltpu.roll(x, 128 - 8 * f, 1) if f else x

    def rows(i, carry):
        tile(pl.multiple_of(i * 8 + TOP, 8), 1.0)
        return carry

    lax.fori_loop(0, ROWS // 8, rows, 0)
    tile(TOP - 8, has_s)
    tile(TOP + ROWS, has_n)


def subcycle_rows(F, r, n):
    lane = lanes(n)
    not_last, not_first = lane < 127, lane > 0
    at = lambda f, j, off=0: F[f][j, pl.ds(r + off, n), :]
    u = [at(U, j) for j in range(5)]
    v = [at(V, j) for j in range(5)]
    ru = [pltpu.roll(x, 127, 1) for x in u]
    rv = [pltpu.roll(x, 127, 1) for x in v]
    n1, n2, sh = [], [], []
    for j in range(5):
        k = (j + 1) % 5
        un, vn = at(U, j, 1), at(V, j, 1)
        ue = jnp.where(not_last, ru[j], ru[k])
        ve = jnp.where(not_last, rv[j], rv[k])
        a = ue - u[j]
        b = vn - v[j]
        shear = (un - u[j]) + (ve - v[j])
        div = a + b
        ten = a - b
        q = div * div + 0.25 * (ten * ten + shear * shear) + 0.01
        s = at(S, j)
        t = s * lax.rsqrt(q)
        t4 = 0.25 * t
        g = t * div - s
        h = t4 * ten
        n1.append(KEEP * at(N1, j) + (g + h))
        n2.append(KEEP * at(N2, j) + (g - h))
        sh.append(KEEP * at(SH, j) + t4 * shear)
    for j in range(5):
        F[N1][j, pl.ds(r, n), :] = n1[j]
        F[N2][j, pl.ds(r, n), :] = n2[j]
        F[SH][j, pl.ds(r, n), :] = sh[j]
    r1 = [pltpu.roll(x, 1, 1) for x in n1]
    r3 = [pltpu.roll(x, 1, 1) for x in sh]
    for j in range(5):
        k = (j + 4) % 5
        n1w = jnp.where(not_first, r1[j], r1[k])
        shw = jnp.where(not_first, r3[j], r3[k])
        fx = (n1[j] - n1w) + (sh[j] - at(SH, j, -1))
        fy = (sh[j] - shw) + (n2[j] - at(N2, j, -1))
        w = at(B, j)
        keep = 1.0 - 0.5 * w
        F[U][j, pl.ds(r, n), :] = keep * (u[j] + 0.3 * v[j]) + (w * fx + at(DE, j))
        F[V][j, pl.ds(r, n), :] = keep * (v[j] - 0.3 * u[j]) + (w * fy + at(DN, j))


def subcycles(F):
    def one(_, carry):
        def rows(i, c):
            for t in range(3):
                subcycle_rows(F, pl.multiple_of(TOP - 8 + 16 * (3 * i + t), 8), 16)
            return c

        lax.fori_loop(0, (ROWS + 16) // 48, rows, 0)
        return carry

    lax.fori_loop(0, SUBCYCLES, one, 0)


def placing(own, place):
    owner = jnp.concatenate(
        [jnp.broadcast_to(own[:, c : c + 1], (8, 128)) for c in range(32)], axis=0
    )
    hot = jnp.where(owner == lanes(256), 1.0, 0.0)
    row = lax.broadcasted_iota(jnp.int32, (256, 256), 0)
    col = lax.broadcasted_iota(jnp.int32, (256, 256), 1)
    before = (col % 8) * 32 + col // 8 < (row % 8) * 32 + row // 8
    before = jnp.where(before, 1.0, 0.0).astype(jnp.bfloat16)
    ranks = jnp.dot(before, hot.astype(jnp.bfloat16), preferred_element_type=jnp.float32)
    rank = jnp.sum(hot * ranks, axis=1, keepdims=True)
    slot = owner.astype(jnp.float32) * 16.0 + rank
    slot = jnp.concatenate([slot, slot], axis=1)
    chosen = jnp.where(slot == col.astype(jnp.float32), 1.0, 0.0)
    place[...] = chosen.T.astype(jnp.bfloat16)


def flatten_blocks(F, blocks):
    group = lanes() // 16
    odd = [(group // 2**t) % 2 == 1 for t in range(3)]
    for c in (U, V):
        for j in range(4):
            for h in range(2):
                x = [F[c][j, pl.ds(TOP + 8 * h + r, 8, stride=16), :] for r in range(8)]
                x = [pltpu.roll(y, 16 * r, 1) if r else y for r, y in enumerate(x)]
                for t in range(3):
                    x = [jnp.where(odd[t], x[(m + 2**t) % 8], x[m]) for m in range(8)]
                for b in range(8):
                    y = x[(8 - b) % 8]
                    y = pltpu.roll(y, 128 - 16 * b, 1) if b else y
                    blocks[pl.ds((8 * j + b) * 8, 8), pl.ds((2 * c + h) * 128, 128)] = y


def gather_blocks(place, blocks, send):
    p = place[...]
    for c in range(2):
        x = blocks[:, pl.ds(256 * c, 256)]
        out = None
        for _ in range(3):
            part = x.astype(jnp.bfloat16)
            term = jnp.dot(p, part, preferred_element_type=jnp.float32)
            out = term if out is None else out + term
            x = x - part.astype(jnp.float32)
        send[c] = out


def dynamics(
    vol_ref, area_ref, vel_ref, forc_ref, cur_ref, strs_ref, mask_ref, own_ref,
    stress_out, vel_out,
    vol, area, vel, forc, cur, strs, mask, own,
    f0, f1, f2, f3, f4, f5, f6, f7, f8,
    W, WE, WW, send_n, send_s, recv_s, recv_n,
    place, blocks, send,
    in_sem, halo_send, halo_recv, out_send, out_recv, own_sem,
):
    F = (f0, f1, f2, f3, f4, f5, f6, f7, f8)
    gx, gy = lax.axis_index("gx"), lax.axis_index("gy")
    n_gx, n_gy = lax.axis_size("gx"), lax.axis_size("gy")
    east, west = lax.rem(gx + 1, n_gx), lax.rem(gx + n_gx - 1, n_gx)
    north, south = lax.rem(gy + 1, n_gy), lax.rem(gy + n_gy - 1, n_gy)

    raw = (vol, area, vel, forc, cur, strs, mask, own)
    sources = (vol_ref, area_ref, vel_ref, forc_ref, cur_ref, strs_ref, mask_ref, own_ref)
    loads = []
    for k, (src, dst) in enumerate(zip(sources, raw)):
        copy = pltpu.make_async_copy(src, dst, in_sem.at[k])
        copy.start()
        loads.append(copy)

    barrier = pltpu.get_barrier_semaphore()
    greeted = [(gx, lax.rem(gy + k, n_gy)) for k in range(1, 16)]
    greeted += [(x, y) for x in (east, west) for y in (gy, north, south)]
    for device in greeted:
        pl.semaphore_signal(barrier, inc=1, device_id=device, device_id_type=MESH)

    for f in F:
        for j in range(5):
            f[j, pl.ds(0, 8), :] = jnp.zeros((8, 128), jnp.float32)
            f[j, pl.ds(HIGH - 8, 8), :] = jnp.zeros((8, 128), jnp.float32)
    for copy in loads:
        copy.wait()
    prepare(raw[:7], F)
    pack_lat(F, send_n, send_s)
    pack_lon(F, W)
    pl.semaphore_wait(barrier, len(greeted))

    first, last = W.at[pl.ds(0, 8), :], W.at[pl.ds(ROWS - 8, 8), :]
    above, below, same = pl.ds(TOP + ROWS, 8), pl.ds(TOP - 8, 8), pl.ds(TOP, ROWS)
    halos = (
        (send_n, recv_s, (gx, north)),
        (send_s, recv_n, (gx, south)),
        (W, WW.at[same, :], (east, gy)),
        (W, WE.at[same, :], (west, gy)),
        (first, WW.at[above, :], (east, south)),
        (first, WE.at[above, :], (west, south)),
        (last, WW.at[below, :], (east, north)),
        (last, WE.at[below, :], (west, north)),
    )
    copies = []
    for k, (src, dst, device) in enumerate(halos):
        copy = pltpu.make_async_remote_copy(
            src_ref=src,
            dst_ref=dst,
            send_sem=halo_send.at[k],
            recv_sem=halo_recv.at[k],
            device_id=device,
            device_id_type=MESH,
        )
        copy.start()
        copies.append(copy)

    placing(own, place)

    for copy in copies:
        copy.wait_recv()
    one, zero = jnp.float32(1.0), jnp.float32(0.0)
    has_e, has_w = jnp.where(gx < n_gx - 1, one, zero), jnp.where(gx > 0, one, zero)
    has_n, has_s = jnp.where(gy < n_gy - 1, one, zero), jnp.where(gy > 0, one, zero)
    unpack_lat(F, recv_s, recv_n, has_s, has_n)
    unpack_lon(F, WE, WW, has_e, has_w, has_s, has_n)

    subcycles(F)
    flatten_blocks(F, blocks)
    gather_blocks(place, blocks, send)

    z, x = gy // 4, lax.rem(gy, 4)
    mine = pl.ds(pl.multiple_of(gy * 16, 16), 16)
    for k, (dz, dx) in enumerate(PEERS):
        to = lax.rem(z + dz, 4) * 4 + lax.rem(x + dx, 4)
        copy = pltpu.make_async_remote_copy(
            src_ref=send.at[:, pl.ds(pl.multiple_of(to * 16, 16), 16), :],
            dst_ref=vel_out.at[:, mine, :],
            send_sem=out_send.at[k],
            recv_sem=out_recv.at[k],
            device_id=(gx, to),
            device_id_type=MESH,
        )
        copy.start()
        copies.append(copy)
    local = pltpu.make_async_copy(send.at[:, mine, :], vel_out.at[:, mine, :], own_sem.at[0])
    local.start()

    def rows(i, carry):
        src = pl.ds(pl.multiple_of(i * 8 + TOP, 8), 8)
        dst = pl.ds(pl.multiple_of(i * 8, 8), 8)
        for j in range(4):
            col = pl.ds(j * 128, 128)
            stress_out[0, dst, col] = F[N1][j, src, :] + F[N2][j, src, :]
            stress_out[1, dst, col] = F[N1][j, src, :] - F[N2][j, src, :]
            stress_out[2, dst, col] = F[SH][j, src, :]
        return carry

    lax.fori_loop(0, ROWS // 8, rows, 0)

    for copy in copies:
        copy.wait_send()
    for copy in copies[len(halos) :]:
        copy.wait_recv()
    local.wait()


def write_out(stress, vel, stress_out, vel_out, sem):
    copies = [
        pltpu.make_async_copy(stress, stress_out, sem.at[0]),
        pltpu.make_async_copy(vel, vel_out, sem.at[1]),
    ]
    for copy in copies:
        copy.start()
    for copy in copies:
        copy.wait()


def per_device(ice_volume, ice_area, velocity, forcing, current, stress, ice_mask, block_owner):
    f32, dma, vmem = jnp.float32, pltpu.SemaphoreType.DMA, pltpu.VMEM
    args = (ice_volume, ice_area, velocity, forcing, current, stress, ice_mask, block_owner)
    args = [pltpu.with_memory_space_constraint(a, pltpu.HBM) for a in args]
    stress_shape, vel_shape = (3, ROWS, COLS), (2, 256, 256)
    scratch = [vmem(a.shape, a.dtype) for a in args]
    scratch += [vmem((5, HIGH, 128), f32)] * 9
    scratch += [vmem((ROWS, 128), f32), vmem((HIGH, 128), f32), vmem((HIGH, 128), f32)]
    scratch += [vmem((5, 4, 8, 128), f32)] * 4
    scratch += [vmem((256, 256), jnp.bfloat16), vmem((256, 512), f32), vmem(vel_shape, f32)]
    scratch += [dma((8,)), dma((8,)), dma((8,)), dma((15,)), dma((15,)), dma((1,))]
    held_stress, held_vel = pl.pallas_call(
        dynamics,
        out_shape=(vmem(stress_shape, f32), vmem(vel_shape, f32)),
        in_specs=[pl.BlockSpec(memory_space=pltpu.HBM)] * 8,
        out_specs=(pl.BlockSpec(memory_space=vmem),) * 2,
        scratch_shapes=scratch,
        compiler_params=pltpu.CompilerParams(
            collective_id=0, has_side_effects=True, vmem_limit_bytes=48 * 2**20
        ),
    )(*args)
    held_stress = pltpu.with_memory_space_constraint(held_stress, vmem)
    held_vel = pltpu.with_memory_space_constraint(held_vel, vmem)
    stress_out, vel_out = pl.pallas_call(
        write_out,
        out_shape=(
            jax.ShapeDtypeStruct(stress_shape, f32),
            jax.ShapeDtypeStruct(vel_shape, f32),
        ),
        in_specs=[pl.BlockSpec(memory_space=vmem)] * 2,
        out_specs=(pl.BlockSpec(memory_space=pl.ANY),) * 2,
        scratch_shapes=[dma((2,))],
    )(held_stress, held_vel)
    return (stress_out, vel_out[:, None])


def solution(mesh):
    tile = P(None, "gy", "gx")
    in_specs = (tile,) * 6 + (P("gy", "gx"),) * 2
    out_specs = (tile, P(None, "gx", "gy", None))
    return jax.shard_map(
        per_device, mesh=mesh, in_specs=in_specs, out_specs=out_specs, check_vma=False
    )
```

time: 128 us -> 30.8 us (0.24)
  starting transfers between devices: 43.9 us -> 0 us
  Pallas kernels: 0 us -> 30 us
  waiting for transfers between devices: 25 us -> 0 us
  blocking collectives: 23.9 us -> 0 us
  other arithmetic: 20.5 us -> 0 us
  local copies, waits for them, and re-layouts: 12.4 us -> 0 us
    ppermute x16 -> x0, starting transfers between devices: 43.9 us -> none  [from_behind(): lax.ppermute(value, axis, [(source, source + steps) for source in range(i...]
    pallas_call x0 -> x2, Pallas kernels: none -> 30 us  [the longest x1 28.9 us: per_device(): pl.pallas_call(dynamics, out_shape=(vmem(stress_shape, f32), vmem(vel_sha...]
    ppermute x16 -> x0, waiting for transfers between devices: 25 us -> none  [from_behind(): lax.ppermute(value, axis, [(source, source + steps) for source in range(i...]
    all_to_all x1 -> x0, blocking collectives: 23.9 us -> none  [per_device(): lax.all_to_all(outgoing_vel, 'gy', split_axis=0, concat_axis=0, tiled=True)]
    another operation x31 -> x0, other arithmetic: 7.8 us -> none  [the longest x12 3.67 us: per_device(): stacked = jnp.stack([normal_east, normal_north, sig_shear])]
    mul x10 -> x0, other arithmetic: 5.15 us -> none  [the longest x4 3.28 us: momentum_half(): (mass * vel_east + force_east + drive_east + CORIOLIS * mass * vel_north)...]
    transpose x1 -> x0, other arithmetic: 4.24 us -> none  [to_blocks(): tile.reshape(channels, block_rows, BLOCK, block_cols, BLOCK)]
    another operation x3 -> x0, local copies, waits for them, and re-layouts: 3.79 us -> none  [the longest x2 3.79 us: per_device(): jnp.stack([vel_east, vel_north])]
  transfers between devices with their start and end apart: 16 -> 0, of which waited for: 7 -> 0; matrix products, arithmetic and copies ran while one was open for 5% -> 0% of each run, Pallas kernels for 0% -> 0%
where the time goes in v1:
time: 30.8 us; the launch traced here: 30.6 us
  Pallas kernels  30 us (97%)
  between operations  0.64 us (2%)
    pallas_call x1, Pallas kernels, per_device(): pl.pallas_call(dynamics, out_shape=(vmem(stress_shape, f32), vmem(vel_sha...  28.9 us
    pallas_call x1, Pallas kernels, per_device(): pl.pallas_call(write_out, out_shape=(jax.ShapeDtypeStruct(stress_shape, f...  1.07 us

profile of v1, /device:TPU:1, one launch (start us, length us, event | category | flops | bytes accessed | tf_op | source)
XLA Modules:
  0.0 30.6 jit_solution(17538519988538553643)
XLA Ops:
  0.6 28.9 %shard_map.95 = (f32[3,128,512]{2,1,0:T(8,128)S(1)}, f32[2,256,256]{2,1,0:T(8,128)S(1)}) custom-call(f32[5,128,512]{2,1,0:T(8,128)} %vol_ref.1, f32[5,128,512]{2,1,0:T(8,128)} %area_ref.1, f32[2,128,512]{2,1,0:T(8,128)} %vel_ref.1, f32[2,128,512]{2,1,0:T(8,128)} %forc_ref.1, f32[2,128,512]{2,1,0:T(8,128)} %cur_ref.1, f32[3,128,512]{2,1,0:T(8,128)} %strs_ref.1, ...), custom_call_target="tpu_custom_call" | custom-call | tf_op jit(solution)/shard_map/pallas_call | solution.py:363
  29.6 1.1 %shard_map.96 = (f32[3,128,512]{2,1,0:T(8,128)}, f32[2,256,256]{2,1,0:T(8,128)}) custom-call(f32[3,128,512]{2,1,0:T(8,128)S(1)} %get-tuple-element.6.stress, f32[2,256,256]{2,1,0:T(8,128)S(1)} %get-tuple-element.7.vel), custom_call_target="tpu_custom_call" | custom-call | tf_op jit(solution)/shard_map/pallas_call | solution.py:375

commit v2 on v1

--- a/solution.py
+++ b/solution.py
@@ -29,13 +29,16 @@
     return lax.broadcasted_iota(jnp.int32, (8, 128), 0)
 
 
-def prepare(raw, F):
-    vol, area, vel, forc, cur, strs, mask = raw
+def prepare(raw, F, first, count, step, n, tiles):
+    held, mask = raw
+    vol, area, vel = held.at[0:5], held.at[5:10], held.at[10:12]
+    forc, cur, strs = held.at[12:14], held.at[14:16], held.at[16:19]
 
     def rows(i, carry):
-        src = pl.ds(pl.multiple_of(i * 8, 8), 8)
-        dst = pl.ds(pl.multiple_of(i * 8 + TOP, 8), 8)
-        for j in range(4):
+        row = first + step * i
+        src = pl.ds(pl.multiple_of(row, 8), n)
+        dst = pl.ds(pl.multiple_of(row + TOP, 8), n)
+        for j in tiles:
             col = pl.ds(j * 128, 128)
             m = mask[src, col].astype(jnp.float32)
             v = [vol[c, src, col] for c in range(5)]
@@ -56,24 +59,25 @@
             F[SH][j, dst, :] = strs[2, src, col] * m
         return carry
 
-    lax.fori_loop(0, ROWS // 8, rows, 0)
+    lax.fori_loop(0, count, rows, 0, unroll=count == 2 and n == 8)
 
 
 def pack_lon(F, W):
-    lane = lanes()
+    n = 64
+    lane = lanes(n)
 
     def rows(i, carry):
-        src = pl.ds(pl.multiple_of(i * 8 + TOP, 8), 8)
-        out = jnp.zeros((8, 128), jnp.float32)
+        src = pl.ds(pl.multiple_of(i * n + TOP, 8), n)
+        out = jnp.zeros((n, 128), jnp.float32)
         for f in range(9):
             x = jnp.where(lane < 64, F[f][0, src, :], F[f][3, src, :])
             x = pltpu.roll(x, 8 * f, 1) if f else x
             here = (lane < 8 * f + 4) & (lane >= 8 * f - 4) if f else (lane < 4) | (lane >= 124)
             out = jnp.where(here, x, out)
-        W[pl.ds(pl.multiple_of(i * 8, 8), 8), :] = out
+        W[pl.ds(pl.multiple_of(i * n, 8), n), :] = out
         return carry
 
-    lax.fori_loop(0, ROWS // 8, rows, 0)
+    lax.fori_loop(0, ROWS // n, rows, 0)
 
 
 def pack_lat(F, send_n, send_s):
@@ -87,12 +91,12 @@
             send_s[p, j] = jnp.where(low, F[f][j, first, :], pltpu.roll(F[g][j, first, :], 4, 0))
 
 
-def unpack_lat(F, recv_s, recv_n, has_s, has_n):
+def unpack_lat(F, recv_s, recv_n):
     for p in range(5):
         f, g = 2 * p, 2 * p + 1
         for j in range(4):
-            x = recv_s[p, j] * has_s
-            y = recv_n[p, j] * has_n
+            x = recv_s[p, j]
+            y = recv_n[p, j]
             F[f][j, pl.ds(TOP - 8, 8), :] = pltpu.roll(x, 4, 0)
             F[f][j, pl.ds(TOP + ROWS, 8), :] = y
             if g < 9:
@@ -100,22 +104,18 @@
                 F[g][j, pl.ds(TOP + ROWS, 8), :] = pltpu.roll(y, 4, 0)
 
 
-def unpack_lon(F, WE, WW, has_e, has_w, has_s, has_n):
-    ahead = lanes() % 8 < 4
-
-    def tile(r, factor):
-        src = pl.ds(r, 8)
-        x = jnp.where(ahead, WE[src, :] * (has_e * factor), WW[src, :] * (has_w * factor))
+def unpack_lon(F, WE, WW):
+    n = 48
+    ahead = lanes(n) % 8 < 4
+
+    def rows(i, carry):
+        src = pl.ds(pl.multiple_of(i * n + TOP - 8, 8), n)
+        x = jnp.where(ahead, WE[src, :], WW[src, :])
         for f in range(9):
             F[f][4, src, :] = pltpu.roll(x, 128 - 8 * f, 1) if f else x
-
-    def rows(i, carry):
-        tile(pl.multiple_of(i * 8 + TOP, 8), 1.0)
         return carry
 
-    lax.fori_loop(0, ROWS // 8, rows, 0)
-    tile(TOP - 8, has_s)
-    tile(TOP + ROWS, has_n)
+    lax.fori_loop(0, (ROWS + 16) // n, rows, 0)
 
 
 def subcycle_rows(F, r, n):
@@ -226,11 +226,11 @@
 def dynamics(
     vol_ref, area_ref, vel_ref, forc_ref, cur_ref, strs_ref, mask_ref, own_ref,
     stress_out, vel_out,
-    vol, area, vel, forc, cur, strs, mask, own,
+    held, mask, own,
     f0, f1, f2, f3, f4, f5, f6, f7, f8,
     W, WE, WW, send_n, send_s, recv_s, recv_n,
     place, blocks, send,
-    in_sem, halo_send, halo_recv, out_send, out_recv, own_sem,
+    in_sem, halo_send, halo_recv, out_sem,
 ):
     F = (f0, f1, f2, f3, f4, f5, f6, f7, f8)
     gx, gy = lax.axis_index("gx"), lax.axis_index("gy")
@@ -238,46 +238,86 @@
     east, west = lax.rem(gx + 1, n_gx), lax.rem(gx + n_gx - 1, n_gx)
     north, south = lax.rem(gy + 1, n_gy), lax.rem(gy + n_gy - 1, n_gy)
 
-    raw = (vol, area, vel, forc, cur, strs, mask, own)
-    sources = (vol_ref, area_ref, vel_ref, forc_ref, cur_ref, strs_ref, mask_ref, own_ref)
+    has_e, has_w, has_n, has_s = gx < n_gx - 1, gx > 0, gy < n_gy - 1, gy > 0
+
+    barrier = pltpu.get_barrier_semaphore()
+    around = (
+        (has_e, (east, gy)),
+        (has_w, (west, gy)),
+        (has_e & has_n, (east, north)),
+        (has_e & has_s, (east, south)),
+        (has_w & has_n, (west, north)),
+        (has_w & has_s, (west, south)),
+    )
+    for there, device in around:
+
+        @pl.when(there)
+        def _(device=device):
+            pl.semaphore_signal(barrier, inc=1, device_id=device, device_id_type=MESH)
+
+    for k in range(1, 16):
+        pl.semaphore_signal(
+            barrier, inc=1, device_id=(gx, lax.rem(gy + k, n_gy)), device_id_type=MESH
+        )
+    one, zero = jnp.int32(1), jnp.int32(0)
+    count = lambda there: jnp.where(there, one, zero)
+    greeted = 15 + (count(has_e) + count(has_w)) * (1 + count(has_n) + count(has_s))
+
+    mask_load = pltpu.make_async_copy(mask_ref, mask, in_sem.at[5])
+    own_load = pltpu.make_async_copy(own_ref, own, in_sem.at[6])
+    mask_load.start()
+    every, inner = pl.ds(0, COLS), pl.ds(8, ROWS - 16)
+    parts = (
+        (pl.ds(0, 8), every),
+        (pl.ds(ROWS - 8, 8), every),
+        (inner, pl.ds(0, 128)),
+        (inner, pl.ds(COLS - 128, 128)),
+        (inner, pl.ds(128, COLS - 256)),
+    )
+    sources = (vol_ref, area_ref, vel_ref, forc_ref, cur_ref, strs_ref)
     loads = []
-    for k, (src, dst) in enumerate(zip(sources, raw)):
-        copy = pltpu.make_async_copy(src, dst, in_sem.at[k])
-        copy.start()
-        loads.append(copy)
-
-    barrier = pltpu.get_barrier_semaphore()
-    greeted = [(gx, lax.rem(gy + k, n_gy)) for k in range(1, 16)]
-    greeted += [(x, y) for x in (east, west) for y in (gy, north, south)]
-    for device in greeted:
-        pl.semaphore_signal(barrier, inc=1, device_id=device, device_id_type=MESH)
+    for k, (r, c) in enumerate(parts):
+        start = 0
+        for src in sources:
+            dst = held.at[pl.ds(start, src.shape[0]), r, c]
+            pltpu.make_async_copy(src.at[:, r, c], dst, in_sem.at[k]).start()
+            start += src.shape[0]
+        loads.append(pltpu.make_async_copy(held.at[:, r, c], held.at[:, r, c], in_sem.at[k]))
+    own_load.start()
 
     for f in F:
         for j in range(5):
             f[j, pl.ds(0, 8), :] = jnp.zeros((8, 128), jnp.float32)
             f[j, pl.ds(HIGH - 8, 8), :] = jnp.zeros((8, 128), jnp.float32)
-    for copy in loads:
-        copy.wait()
-    prepare(raw[:7], F)
-    pack_lat(F, send_n, send_s)
-    pack_lon(F, W)
-    pl.semaphore_wait(barrier, len(greeted))
+    above, below, same = pl.ds(TOP + ROWS, 8), pl.ds(TOP - 8, 8), pl.ds(TOP, ROWS)
+    for there, buf in ((has_s, recv_s), (has_n, recv_n)):
+
+        @pl.when(jnp.logical_not(there))
+        def _(buf=buf):
+            buf[...] = jnp.zeros(buf.shape, jnp.float32)
+
+    for there, buf in ((has_e, WE), (has_w, WW)):
+        for beside, at in ((has_n, above), (has_s, below), (there, same)):
+
+            @pl.when(jnp.logical_not(there & beside))
+            def _(buf=buf, at=at):
+                buf[at, :] = jnp.zeros((at.size, 128), jnp.float32)
 
     first, last = W.at[pl.ds(0, 8), :], W.at[pl.ds(ROWS - 8, 8), :]
-    above, below, same = pl.ds(TOP + ROWS, 8), pl.ds(TOP - 8, 8), pl.ds(TOP, ROWS)
     halos = (
-        (send_n, recv_s, (gx, north)),
-        (send_s, recv_n, (gx, south)),
-        (W, WW.at[same, :], (east, gy)),
-        (W, WE.at[same, :], (west, gy)),
-        (first, WW.at[above, :], (east, south)),
-        (first, WE.at[above, :], (west, south)),
-        (last, WW.at[below, :], (east, north)),
-        (last, WE.at[below, :], (west, north)),
+        (send_n, recv_s, (gx, north), has_n, has_s),
+        (send_s, recv_n, (gx, south), has_s, has_n),
+        (W, WW.at[same, :], (east, gy), has_e, has_w),
+        (W, WE.at[same, :], (west, gy), has_w, has_e),
+        (first, WW.at[above, :], (east, south), has_e & has_s, has_w & has_n),
+        (first, WE.at[above, :], (west, south), has_w & has_s, has_e & has_n),
+        (last, WW.at[below, :], (east, north), has_e & has_n, has_w & has_s),
+        (last, WE.at[below, :], (west, north), has_w & has_n, has_e & has_s),
     )
-    copies = []
-    for k, (src, dst, device) in enumerate(halos):
-        copy = pltpu.make_async_remote_copy(
+
+    def halo(k):
+        src, dst, device, _, _ = halos[k]
+        return pltpu.make_async_remote_copy(
             src_ref=src,
             dst_ref=dst,
             send_sem=halo_send.at[k],
@@ -285,18 +325,41 @@
             device_id=device,
             device_id_type=MESH,
         )
-        copy.start()
-        copies.append(copy)
-
+
+    def start_halo(k):
+        @pl.when(halos[k][3])
+        def _():
+            halo(k).start()
+
+    mask_load.wait()
+    loads[0].wait()
+    loads[1].wait()
+    prepare((held, mask), F, 0, 2, ROWS - 8, 8, range(4))
+    pack_lat(F, send_n, send_s)
+    pl.semaphore_wait(barrier, greeted)
+    for k in (0, 1):
+        start_halo(k)
+
+    loads[2].wait()
+    loads[3].wait()
+    prepare((held, mask), F, 8, 2, 56, 56, (0, 3))
+    pack_lon(F, W)
+    for k in range(2, 8):
+        start_halo(k)
+
+    loads[4].wait()
+    prepare((held, mask), F, 8, 2, 56, 56, (1, 2))
+    own_load.wait()
     placing(own, place)
 
-    for copy in copies:
-        copy.wait_recv()
-    one, zero = jnp.float32(1.0), jnp.float32(0.0)
-    has_e, has_w = jnp.where(gx < n_gx - 1, one, zero), jnp.where(gx > 0, one, zero)
-    has_n, has_s = jnp.where(gy < n_gy - 1, one, zero), jnp.where(gy > 0, one, zero)
-    unpack_lat(F, recv_s, recv_n, has_s, has_n)
-    unpack_lon(F, WE, WW, has_e, has_w, has_s, has_n)
+    for k in range(8):
+
+        @pl.when(halos[k][4])
+        def _(k=k):
+            halo(k).wait_recv()
+
+    unpack_lat(F, recv_s, recv_n)
+    unpack_lon(F, WE, WW)
 
     subcycles(F)
     flatten_blocks(F, blocks)
@@ -304,24 +367,23 @@
 
     z, x = gy // 4, lax.rem(gy, 4)
     mine = pl.ds(pl.multiple_of(gy * 16, 16), 16)
-    for k, (dz, dx) in enumerate(PEERS):
+    for dz, dx in PEERS:
         to = lax.rem(z + dz, 4) * 4 + lax.rem(x + dx, 4)
         copy = pltpu.make_async_remote_copy(
             src_ref=send.at[:, pl.ds(pl.multiple_of(to * 16, 16), 16), :],
             dst_ref=vel_out.at[:, mine, :],
-            send_sem=out_send.at[k],
-            recv_sem=out_recv.at[k],
+            send_sem=out_sem.at[0],
+            recv_sem=out_sem.at[1],
             device_id=(gx, to),
             device_id_type=MESH,
         )
         copy.start()
-        copies.append(copy)
-    local = pltpu.make_async_copy(send.at[:, mine, :], vel_out.at[:, mine, :], own_sem.at[0])
+    local = pltpu.make_async_copy(send.at[:, mine, :], vel_out.at[:, mine, :], out_sem.at[2])
     local.start()
 
     def rows(i, carry):
-        src = pl.ds(pl.multiple_of(i * 8 + TOP, 8), 8)
-        dst = pl.ds(pl.multiple_of(i * 8, 8), 8)
+        src = pl.ds(pl.multiple_of(i * 16 + TOP, 8), 16)
+        dst = pl.ds(pl.multiple_of(i * 16, 8), 16)
         for j in range(4):
             col = pl.ds(j * 128, 128)
             stress_out[0, dst, col] = F[N1][j, src, :] + F[N2][j, src, :]
@@ -329,12 +391,17 @@
             stress_out[2, dst, col] = F[SH][j, src, :]
         return carry
 
-    lax.fori_loop(0, ROWS // 8, rows, 0)
-
-    for copy in copies:
-        copy.wait_send()
-    for copy in copies[len(halos) :]:
-        copy.wait_recv()
+    lax.fori_loop(0, ROWS // 16, rows, 0)
+
+    for k in range(8):
+
+        @pl.when(halos[k][3])
+        def _(k=k):
+            halo(k).wait_send()
+
+    others = pl.ds(0, 240)
+    for k in range(2):
+        pltpu.make_async_copy(send.at[:, others, :], vel_out.at[:, others, :], out_sem.at[k]).wait()
     local.wait()
 
 
@@ -354,12 +421,12 @@
     args = (ice_volume, ice_area, velocity, forcing, current, stress, ice_mask, block_owner)
     args = [pltpu.with_memory_space_constraint(a, pltpu.HBM) for a in args]
     stress_shape, vel_shape = (3, ROWS, COLS), (2, 256, 256)
-    scratch = [vmem(a.shape, a.dtype) for a in args]
+    scratch = [vmem((19, ROWS, COLS), f32)] + [vmem(a.shape, a.dtype) for a in args[6:]]
     scratch += [vmem((5, HIGH, 128), f32)] * 9
     scratch += [vmem((ROWS, 128), f32), vmem((HIGH, 128), f32), vmem((HIGH, 128), f32)]
     scratch += [vmem((5, 4, 8, 128), f32)] * 4
     scratch += [vmem((256, 256), jnp.bfloat16), vmem((256, 512), f32), vmem(vel_shape, f32)]
-    scratch += [dma((8,)), dma((8,)), dma((8,)), dma((15,)), dma((15,)), dma((1,))]
+    scratch += [dma((7,)), dma((8,)), dma((8,)), dma((3,))]
     held_stress, held_vel = pl.pallas_call(
         dynamics,
         out_shape=(vmem(stress_shape, f32), vmem(vel_shape, f32)),

time: 30.8 us -> 27.5 us (0.89)
  Pallas kernels: 30 us -> 26.7 us
    pallas_call x1, Pallas kernels: 28.9 us -> 25.6 us  [per_device(): pl.pallas_call(dynamics, out_shape=(vmem(stress_shape, f32), vmem(vel_sha...]
where the time goes in v2:
time: 27.5 us; the launch traced here: 27.3 us
  Pallas kernels  26.7 us (97%)
  between operations  0.64 us (2%)
    pallas_call x1, Pallas kernels, per_device(): pl.pallas_call(dynamics, out_shape=(vmem(stress_shape, f32), vmem(vel_sha...  25.6 us
    pallas_call x1, Pallas kernels, per_device(): pl.pallas_call(write_out, out_shape=(jax.ShapeDtypeStruct(stress_shape, f...  1.07 us

profile of v2, /device:TPU:1, one launch (start us, length us, event | category | flops | bytes accessed | tf_op | source)
XLA Modules:
  0.0 27.3 jit_solution(6006740965742295001)
XLA Ops:
  0.6 25.6 %shard_map.95 = (f32[3,128,512]{2,1,0:T(8,128)S(1)}, f32[2,256,256]{2,1,0:T(8,128)S(1)}) custom-call(f32[5,128,512]{2,1,0:T(8,128)} %vol_ref.1, f32[5,128,512]{2,1,0:T(8,128)} %area_ref.1, f32[2,128,512]{2,1,0:T(8,128)} %vel_ref.1, f32[2,128,512]{2,1,0:T(8,128)} %forc_ref.1, f32[2,128,512]{2,1,0:T(8,128)} %cur_ref.1, f32[3,128,512]{2,1,0:T(8,128)} %strs_ref.1, ...), custom_call_target="tpu_custom_call" | custom-call | tf_op jit(solution)/shard_map/pallas_call | solution.py:430
  26.3 1.1 %shard_map.96 = (f32[3,128,512]{2,1,0:T(8,128)}, f32[2,256,256]{2,1,0:T(8,128)}) custom-call(f32[3,128,512]{2,1,0:T(8,128)S(1)} %get-tuple-element.6.stress, f32[2,256,256]{2,1,0:T(8,128)S(1)} %get-tuple-element.7.vel), custom_call_target="tpu_custom_call" | custom-call | tf_op jit(solution)/shard_map/pallas_call | solution.py:442

commit v3 on v2

--- a/solution.py
+++ b/solution.py
@@ -47,16 +47,15 @@
             conc = ((a[0] + a[1]) + (a[2] + a[3])) + a[4]
             strength = 2.0 * total * jnp.exp(-20.0 * (1.0 - conc))
             weight = m / (total + 1.0)
-            F[S][j, dst, :] = strength * m * (1.0 / 6.0)
-            F[B][j, dst, :] = weight
+            F[S][j, dst, :] = strength * m * (1.0 / 3.0)
+            F[B][j, dst, :] = 0.5 * weight
             F[DE][j, dst, :] = weight * (forc[0, src, col] + 0.5 * cur[0, src, col])
             F[DN][j, dst, :] = weight * (forc[1, src, col] + 0.5 * cur[1, src, col])
             F[U][j, dst, :] = vel[0, src, col] * m
             F[V][j, dst, :] = vel[1, src, col] * m
-            half = 0.5 * m
-            F[N1][j, dst, :] = half * (strs[0, src, col] + strs[1, src, col])
-            F[N2][j, dst, :] = half * (strs[0, src, col] - strs[1, src, col])
-            F[SH][j, dst, :] = strs[2, src, col] * m
+            F[N1][j, dst, :] = m * (strs[0, src, col] + strs[1, src, col])
+            F[N2][j, dst, :] = m * (strs[0, src, col] - strs[1, src, col])
+            F[SH][j, dst, :] = (m + m) * strs[2, src, col]
         return carry
 
     lax.fori_loop(0, count, rows, 0, unroll=count == 2 and n == 8)
@@ -91,50 +90,83 @@
             send_s[p, j] = jnp.where(low, F[f][j, first, :], pltpu.roll(F[g][j, first, :], 4, 0))
 
 
-def unpack_lat(F, recv_s, recv_n):
+def copy_edges(F, T, G):
+    for f in range(9):
+        for j in range(4):
+            T[f][j, pl.ds(16, 8), :] = F[f][j, pl.ds(TOP, 8), :]
+            T[f][j, pl.ds(24, 8), :] = F[f][j, pl.ds(TOP + ROWS - 8, 8), :]
+    n = 64
+
+    def rows(i, carry):
+        at = pl.ds(pl.multiple_of(i * n + TOP, 8), n)
+        for f in range(9):
+            G[f][0, at, :] = edge_columns(F[f][0, at, :], F[f][3, at, :])
+        return carry
+
+    lax.fori_loop(0, ROWS // n, rows, 0)
+
+
+def edge_columns(first, last):
+    lane = lanes(first.shape[0])
+    own = jnp.where(lane < 8, first, 0.0)
+    return jnp.where((lane >= 56) & (lane < 64), pltpu.roll(last, 64, 1), own)
+
+
+def unpack_lat(T, G, recv_s, recv_n):
+    behind, ahead = pl.ds(8, 8), pl.ds(32, 8)
     for p in range(5):
         f, g = 2 * p, 2 * p + 1
         for j in range(4):
             x = recv_s[p, j]
             y = recv_n[p, j]
-            F[f][j, pl.ds(TOP - 8, 8), :] = pltpu.roll(x, 4, 0)
-            F[f][j, pl.ds(TOP + ROWS, 8), :] = y
+            T[f][j, behind, :] = pltpu.roll(x, 4, 0)
+            T[f][j, ahead, :] = y
             if g < 9:
-                F[g][j, pl.ds(TOP - 8, 8), :] = x
-                F[g][j, pl.ds(TOP + ROWS, 8), :] = pltpu.roll(y, 4, 0)
-
-
-def unpack_lon(F, WE, WW):
+                T[g][j, behind, :] = x
+                T[g][j, ahead, :] = pltpu.roll(y, 4, 0)
+    for f in range(9):
+        G[f][0, pl.ds(TOP - 8, 8), :] = edge_columns(T[f][0, behind, :], T[f][3, behind, :])
+        G[f][0, pl.ds(TOP + ROWS, 8), :] = edge_columns(T[f][0, ahead, :], T[f][3, ahead, :])
+
+
+def unpack_lon(G, WE, WW):
     n = 48
-    ahead = lanes(n) % 8 < 4
+    lane = lanes(n)
+    ahead = lane % 8 < 4
+    halo = (lane >= 124) | ((lane >= 64) & (lane < 68))
 
     def rows(i, carry):
         src = pl.ds(pl.multiple_of(i * n + TOP - 8, 8), n)
-        x = jnp.where(ahead, WE[src, :], WW[src, :])
+        x = jnp.where(ahead, pltpu.roll(WE[src, :], 64, 1), WW[src, :])
         for f in range(9):
-            F[f][4, src, :] = pltpu.roll(x, 128 - 8 * f, 1) if f else x
+            y = pltpu.roll(x, 128 - 8 * f, 1) if f else x
+            G[f][0, src, :] = jnp.where(halo, y, G[f][0, src, :])
         return carry
 
     lax.fori_loop(0, (ROWS + 16) // n, rows, 0)
 
 
 def subcycle_rows(F, r, n):
+    tiles = F[0].shape[0]
     lane = lanes(n)
     not_last, not_first = lane < 127, lane > 0
     at = lambda f, j, off=0: F[f][j, pl.ds(r + off, n), :]
-    u = [at(U, j) for j in range(5)]
-    v = [at(V, j) for j in range(5)]
-    ru = [pltpu.roll(x, 127, 1) for x in u]
-    rv = [pltpu.roll(x, 127, 1) for x in v]
+
+    def beside(x, step):
+        turned = [pltpu.roll(y, 127 if step > 0 else 1, 1) for y in x]
+        if tiles == 1:
+            return turned
+        inside = not_last if step > 0 else not_first
+        return [jnp.where(inside, turned[j], turned[(j + step) % tiles]) for j in range(tiles)]
+
+    u = [at(U, j) for j in range(tiles)]
+    v = [at(V, j) for j in range(tiles)]
+    ue, ve = beside(u, 1), beside(v, 1)
     n1, n2, sh = [], [], []
-    for j in range(5):
-        k = (j + 1) % 5
-        un, vn = at(U, j, 1), at(V, j, 1)
-        ue = jnp.where(not_last, ru[j], ru[k])
-        ve = jnp.where(not_last, rv[j], rv[k])
-        a = ue - u[j]
-        b = vn - v[j]
-        shear = (un - u[j]) + (ve - v[j])
+    for j in range(tiles):
+        a = ue[j] - u[j]
+        b = at(V, j, 1) - v[j]
+        shear = (at(U, j, 1) - u[j]) + (ve[j] - v[j])
         div = a + b
         ten = a - b
         q = div * div + 0.25 * (ten * ten + shear * shear) + 0.01
@@ -146,35 +178,58 @@
         n1.append(KEEP * at(N1, j) + (g + h))
         n2.append(KEEP * at(N2, j) + (g - h))
         sh.append(KEEP * at(SH, j) + t4 * shear)
-    for j in range(5):
+    for j in range(tiles):
         F[N1][j, pl.ds(r, n), :] = n1[j]
         F[N2][j, pl.ds(r, n), :] = n2[j]
         F[SH][j, pl.ds(r, n), :] = sh[j]
-    r1 = [pltpu.roll(x, 1, 1) for x in n1]
-    r3 = [pltpu.roll(x, 1, 1) for x in sh]
-    for j in range(5):
-        k = (j + 4) % 5
-        n1w = jnp.where(not_first, r1[j], r1[k])
-        shw = jnp.where(not_first, r3[j], r3[k])
-        fx = (n1[j] - n1w) + (sh[j] - at(SH, j, -1))
-        fy = (sh[j] - shw) + (n2[j] - at(N2, j, -1))
+    n1w, shw = beside(n1, -1), beside(sh, -1)
+    for j in range(tiles):
+        fx = (n1[j] - n1w[j]) + (sh[j] - at(SH, j, -1))
+        fy = (sh[j] - shw[j]) + (n2[j] - at(N2, j, -1))
         w = at(B, j)
-        keep = 1.0 - 0.5 * w
-        F[U][j, pl.ds(r, n), :] = keep * (u[j] + 0.3 * v[j]) + (w * fx + at(DE, j))
-        F[V][j, pl.ds(r, n), :] = keep * (v[j] - 0.3 * u[j]) + (w * fy + at(DN, j))
-
-
-def subcycles(F):
+        x = u[j] + 0.3 * v[j]
+        y = v[j] - 0.3 * u[j]
+        F[U][j, pl.ds(r, n), :] = (x + at(DE, j)) + w * (fx - x)
+        F[V][j, pl.ds(r, n), :] = (y + at(DN, j)) + w * (fy - y)
+
+
+def subcycles_inside(F):
     def one(_, carry):
         def rows(i, c):
-            for t in range(3):
-                subcycle_rows(F, pl.multiple_of(TOP - 8 + 16 * (3 * i + t), 8), 16)
+            for t in range(4):
+                subcycle_rows(F, pl.multiple_of(TOP + 64 * i + 16 * t, 8), 16)
             return c
 
-        lax.fori_loop(0, (ROWS + 16) // 48, rows, 0)
+        lax.fori_loop(0, ROWS // 64, rows, 0)
         return carry
 
     lax.fori_loop(0, SUBCYCLES, one, 0)
+
+
+def subcycles_edges(T, G):
+    def one(_, carry):
+        subcycle_rows(T, 8, 32)
+        for t in range(3):
+            subcycle_rows(G, TOP - 8 + 48 * t, 48)
+        return carry
+
+    lax.fori_loop(0, SUBCYCLES, one, 0)
+
+
+def merge_edges(F, T, G, fields):
+    low = sublanes() < 4
+    for f in fields:
+        for j in range(4):
+            first, last = pl.ds(TOP, 8), pl.ds(TOP + ROWS - 8, 8)
+            F[f][j, first, :] = jnp.where(low, T[f][j, pl.ds(16, 8), :], F[f][j, first, :])
+            F[f][j, last, :] = jnp.where(low, F[f][j, last, :], T[f][j, pl.ds(24, 8), :])
+        n = 64
+        for i in range(ROWS // n):
+            at = pl.ds(TOP + i * n, n)
+            lane = lanes(n)
+            x = G[f][0, at, :]
+            F[f][0, at, :] = jnp.where(lane < 4, x, F[f][0, at, :])
+            F[f][3, at, :] = jnp.where(lane >= 124, pltpu.roll(x, 64, 1), F[f][3, at, :])
 
 
 def placing(own, place):
@@ -228,17 +283,53 @@
     stress_out, vel_out,
     held, mask, own,
     f0, f1, f2, f3, f4, f5, f6, f7, f8,
+    t0, t1, t2, t3, t4, t5, t6, t7, t8,
+    g0, g1, g2, g3, g4, g5, g6, g7, g8,
     W, WE, WW, send_n, send_s, recv_s, recv_n,
     place, blocks, send,
     in_sem, halo_send, halo_recv, out_sem,
 ):
     F = (f0, f1, f2, f3, f4, f5, f6, f7, f8)
+    T = (t0, t1, t2, t3, t4, t5, t6, t7, t8)
+    G = (g0, g1, g2, g3, g4, g5, g6, g7, g8)
     gx, gy = lax.axis_index("gx"), lax.axis_index("gy")
     n_gx, n_gy = lax.axis_size("gx"), lax.axis_size("gy")
     east, west = lax.rem(gx + 1, n_gx), lax.rem(gx + n_gx - 1, n_gx)
     north, south = lax.rem(gy + 1, n_gy), lax.rem(gy + n_gy - 1, n_gy)
 
     has_e, has_w, has_n, has_s = gx < n_gx - 1, gx > 0, gy < n_gy - 1, gy > 0
+
+    every, inner, mid = pl.ds(0, ROWS), pl.ds(8, ROWS - 16), pl.ds(128, COLS - 256)
+    parts = (
+        (every, pl.ds(0, 128)),
+        (every, pl.ds(COLS - 128, 128)),
+        (pl.ds(0, 8), mid),
+        (pl.ds(ROWS - 8, 8), mid),
+        (inner, mid),
+    )
+    sources = (vol_ref, area_ref, vel_ref, forc_ref, cur_ref, strs_ref)
+
+    def start_load(k):
+        r, c = parts[k]
+        start = 0
+        for src in sources:
+            dst = held.at[pl.ds(start, src.shape[0]), r, c]
+            pltpu.make_async_copy(src.at[:, r, c], dst, in_sem.at[k]).start()
+            start += src.shape[0]
+
+    def wait_load(k):
+        at = held.at[:, parts[k][0], parts[k][1]]
+        pltpu.make_async_copy(at, at, in_sem.at[k]).wait()
+
+    masks = [
+        pltpu.make_async_copy(mask_ref.at[:, c], mask.at[:, c], in_sem.at[5 + k])
+        for k, c in enumerate((parts[0][1], parts[1][1], mid))
+    ]
+    own_load = pltpu.make_async_copy(own_ref, own, in_sem.at[8])
+    start_load(0)
+    masks[0].start()
+    start_load(1)
+    masks[1].start()
 
     barrier = pltpu.get_barrier_semaphore()
     around = (
@@ -263,32 +354,17 @@
     count = lambda there: jnp.where(there, one, zero)
     greeted = 15 + (count(has_e) + count(has_w)) * (1 + count(has_n) + count(has_s))
 
-    mask_load = pltpu.make_async_copy(mask_ref, mask, in_sem.at[5])
-    own_load = pltpu.make_async_copy(own_ref, own, in_sem.at[6])
-    mask_load.start()
-    every, inner = pl.ds(0, COLS), pl.ds(8, ROWS - 16)
-    parts = (
-        (pl.ds(0, 8), every),
-        (pl.ds(ROWS - 8, 8), every),
-        (inner, pl.ds(0, 128)),
-        (inner, pl.ds(COLS - 128, 128)),
-        (inner, pl.ds(128, COLS - 256)),
-    )
-    sources = (vol_ref, area_ref, vel_ref, forc_ref, cur_ref, strs_ref)
-    loads = []
-    for k, (r, c) in enumerate(parts):
-        start = 0
-        for src in sources:
-            dst = held.at[pl.ds(start, src.shape[0]), r, c]
-            pltpu.make_async_copy(src.at[:, r, c], dst, in_sem.at[k]).start()
-            start += src.shape[0]
-        loads.append(pltpu.make_async_copy(held.at[:, r, c], held.at[:, r, c], in_sem.at[k]))
+    start_load(2)
+    start_load(3)
+    masks[2].start()
+    start_load(4)
     own_load.start()
 
-    for f in F:
-        for j in range(5):
-            f[j, pl.ds(0, 8), :] = jnp.zeros((8, 128), jnp.float32)
-            f[j, pl.ds(HIGH - 8, 8), :] = jnp.zeros((8, 128), jnp.float32)
+    for buf, tiles, ends in ((F, 4, (8, 144)), (T, 4, (0, 40)), (G, 1, (0, 152))):
+        for f in buf:
+            for j in range(tiles):
+                for r in ends:
+                    f[j, pl.ds(r, 8), :] = jnp.zeros((8, 128), jnp.float32)
     above, below, same = pl.ds(TOP + ROWS, 8), pl.ds(TOP - 8, 8), pl.ds(TOP, ROWS)
     for there, buf in ((has_s, recv_s), (has_n, recv_n)):
 
@@ -331,24 +407,28 @@
         def _():
             halo(k).start()
 
-    mask_load.wait()
-    loads[0].wait()
-    loads[1].wait()
-    prepare((held, mask), F, 0, 2, ROWS - 8, 8, range(4))
+    wait_load(0)
+    masks[0].wait()
+    wait_load(1)
+    masks[1].wait()
+    prepare((held, mask), F, 0, 2, 64, 64, (0, 3))
+    pack_lon(F, W)
+    pl.semaphore_wait(barrier, greeted)
+    for k in range(2, 8):
+        start_halo(k)
+
+    wait_load(2)
+    wait_load(3)
+    masks[2].wait()
+    prepare((held, mask), F, 0, 2, ROWS - 8, 8, (1, 2))
     pack_lat(F, send_n, send_s)
-    pl.semaphore_wait(barrier, greeted)
     for k in (0, 1):
         start_halo(k)
 
-    loads[2].wait()
-    loads[3].wait()
-    prepare((held, mask), F, 8, 2, 56, 56, (0, 3))
-    pack_lon(F, W)
-    for k in range(2, 8):
-        start_halo(k)
-
-    loads[4].wait()
+    wait_load(4)
     prepare((held, mask), F, 8, 2, 56, 56, (1, 2))
+    copy_edges(F, T, G)
+    subcycles_inside(F)
     own_load.wait()
     placing(own, place)
 
@@ -358,10 +438,10 @@
         def _(k=k):
             halo(k).wait_recv()
 
-    unpack_lat(F, recv_s, recv_n)
-    unpack_lon(F, WE, WW)
-
-    subcycles(F)
+    unpack_lat(T, G, recv_s, recv_n)
+    unpack_lon(G, WE, WW)
+    subcycles_edges(T, G)
+    merge_edges(F, T, G, (U, V))
     flatten_blocks(F, blocks)
     gather_blocks(place, blocks, send)
 
@@ -381,14 +461,16 @@
     local = pltpu.make_async_copy(send.at[:, mine, :], vel_out.at[:, mine, :], out_sem.at[2])
     local.start()
 
+    merge_edges(F, T, G, (N1, N2, SH))
+
     def rows(i, carry):
         src = pl.ds(pl.multiple_of(i * 16 + TOP, 8), 16)
         dst = pl.ds(pl.multiple_of(i * 16, 8), 16)
         for j in range(4):
             col = pl.ds(j * 128, 128)
-            stress_out[0, dst, col] = F[N1][j, src, :] + F[N2][j, src, :]
-            stress_out[1, dst, col] = F[N1][j, src, :] - F[N2][j, src, :]
-            stress_out[2, dst, col] = F[SH][j, src, :]
+            stress_out[0, dst, col] = 0.5 * (F[N1][j, src, :] + F[N2][j, src, :])
+            stress_out[1, dst, col] = 0.5 * (F[N1][j, src, :] - F[N2][j, src, :])
+            stress_out[2, dst, col] = 0.5 * F[SH][j, src, :]
         return carry
 
     lax.fori_loop(0, ROWS // 16, rows, 0)
@@ -422,11 +504,12 @@
     args = [pltpu.with_memory_space_constraint(a, pltpu.HBM) for a in args]
     stress_shape, vel_shape = (3, ROWS, COLS), (2, 256, 256)
     scratch = [vmem((19, ROWS, COLS), f32)] + [vmem(a.shape, a.dtype) for a in args[6:]]
-    scratch += [vmem((5, HIGH, 128), f32)] * 9
+    scratch += [vmem((4, HIGH, 128), f32)] * 9 + [vmem((4, 48, 128), f32)] * 9
+    scratch += [vmem((1, HIGH, 128), f32)] * 9
     scratch += [vmem((ROWS, 128), f32), vmem((HIGH, 128), f32), vmem((HIGH, 128), f32)]
     scratch += [vmem((5, 4, 8, 128), f32)] * 4
     scratch += [vmem((256, 256), jnp.bfloat16), vmem((256, 512), f32), vmem(vel_shape, f32)]
-    scratch += [dma((7,)), dma((8,)), dma((8,)), dma((3,))]
+    scratch += [dma((9,)), dma((8,)), dma((8,)), dma((3,))]
     held_stress, held_vel = pl.pallas_call(
         dynamics,
         out_shape=(vmem(stress_shape, f32), vmem(vel_shape, f32)),

time: 27.5 us -> 24.1 us (0.88)
  Pallas kernels: 26.7 us -> 23.4 us
    pallas_call x1, Pallas kernels: 25.6 us -> 22.3 us  [per_device(): pl.pallas_call(dynamics, out_shape=(vmem(stress_shape, f32), vmem(vel_sha...]
where the time goes in v3:
time: 24.1 us; the launch traced here: 24 us
  Pallas kernels  23.4 us (97%)
  between operations  0.64 us (3%)
    pallas_call x1, Pallas kernels, per_device(): pl.pallas_call(dynamics, out_shape=(vmem(stress_shape, f32), vmem(vel_sha...  22.3 us
    pallas_call x1, Pallas kernels, per_device(): pl.pallas_call(write_out, out_shape=(jax.ShapeDtypeStruct(stress_shape, f...  1.07 us

profile of v3, /device:TPU:1, one launch (start us, length us, event | category | flops | bytes accessed | tf_op | source)
XLA Modules:
  0.0 24.0 jit_solution(2016491225715388850)
XLA Ops:
  0.6 22.3 %shard_map.95 = (f32[3,128,512]{2,1,0:T(8,128)S(1)}, f32[2,256,256]{2,1,0:T(8,128)S(1)}) custom-call(f32[5,128,512]{2,1,0:T(8,128)} %vol_ref.1, f32[5,128,512]{2,1,0:T(8,128)} %area_ref.1, f32[2,128,512]{2,1,0:T(8,128)} %vel_ref.1, f32[2,128,512]{2,1,0:T(8,128)} %forc_ref.1, f32[2,128,512]{2,1,0:T(8,128)} %cur_ref.1, f32[3,128,512]{2,1,0:T(8,128)} %strs_ref.1, ...), custom_call_target="tpu_custom_call" | custom-call | tf_op jit(solution)/shard_map/pallas_call | solution.py:513
  23.0 1.1 %shard_map.96 = (f32[3,128,512]{2,1,0:T(8,128)}, f32[2,256,256]{2,1,0:T(8,128)}) custom-call(f32[3,128,512]{2,1,0:T(8,128)S(1)} %get-tuple-element.6.stress, f32[2,256,256]{2,1,0:T(8,128)S(1)} %get-tuple-element.7.vel), custom_call_target="tpu_custom_call" | custom-call | tf_op jit(solution)/shard_map/pallas_call | solution.py:525

commit v4 on v3

--- a/solution.py
+++ b/solution.py
@@ -14,10 +14,7 @@
 TOP = 16
 HIGH = ROWS + 32
 KEEP = 2.0 / 3.0
-PEERS = (
-    (2, 2), (2, 3), (3, 2), (2, 1), (1, 2), (2, 0), (0, 2), (3, 1),
-    (1, 3), (3, 3), (1, 1), (3, 0), (0, 3), (1, 0), (0, 1),
-)
+OWNERS = (0, 1, 4, 3, 2, 5, 8, 7, 6, 9, 12, 11, 10, 13, 15, 14)
 U, V, N1, N2, SH, S, B, DE, DN = range(9)
 
 
@@ -61,22 +58,16 @@
     lax.fori_loop(0, count, rows, 0, unroll=count == 2 and n == 8)
 
 
-def pack_lon(F, W):
-    n = 64
+def pack_lon(F, W, start, n):
     lane = lanes(n)
-
-    def rows(i, carry):
-        src = pl.ds(pl.multiple_of(i * n + TOP, 8), n)
-        out = jnp.zeros((n, 128), jnp.float32)
-        for f in range(9):
-            x = jnp.where(lane < 64, F[f][0, src, :], F[f][3, src, :])
-            x = pltpu.roll(x, 8 * f, 1) if f else x
-            here = (lane < 8 * f + 4) & (lane >= 8 * f - 4) if f else (lane < 4) | (lane >= 124)
-            out = jnp.where(here, x, out)
-        W[pl.ds(pl.multiple_of(i * n, 8), n), :] = out
-        return carry
-
-    lax.fori_loop(0, ROWS // n, rows, 0)
+    src = pl.ds(start + TOP, n)
+    out = jnp.zeros((n, 128), jnp.float32)
+    for f in range(9):
+        x = jnp.where(lane < 64, F[f][0, src, :], F[f][3, src, :])
+        x = pltpu.roll(x, 8 * f, 1) if f else x
+        here = (lane < 8 * f + 4) & (lane >= 8 * f - 4) if f else (lane < 4) | (lane >= 124)
+        out = jnp.where(here, x, out)
+    W[pl.ds(start, n), :] = out
 
 
 def pack_lat(F, send_n, send_s):
@@ -90,60 +81,57 @@
             send_s[p, j] = jnp.where(low, F[f][j, first, :], pltpu.roll(F[g][j, first, :], 4, 0))
 
 
+def turn(x, by):
+    return pltpu.roll(x, by % 128, 1) if by % 128 else x
+
+
+def edge_columns(first, last, q):
+    lane = lanes(first.shape[0])
+    in_east = (lane >= 32 * q) & (lane < 32 * q + 8)
+    in_west = (lane >= 32 * q + 24) & (lane < 32 * q + 32)
+    return in_east, turn(last, 32 * q + 8), in_west, turn(first, 32 * q + 24)
+
+
 def copy_edges(F, T, G):
     for f in range(9):
         for j in range(4):
-            T[f][j, pl.ds(16, 8), :] = F[f][j, pl.ds(TOP, 8), :]
-            T[f][j, pl.ds(24, 8), :] = F[f][j, pl.ds(TOP + ROWS - 8, 8), :]
-    n = 64
-
-    def rows(i, carry):
-        at = pl.ds(pl.multiple_of(i * n + TOP, 8), n)
-        for f in range(9):
-            G[f][0, at, :] = edge_columns(F[f][0, at, :], F[f][3, at, :])
-        return carry
-
-    lax.fori_loop(0, ROWS // n, rows, 0)
-
-
-def edge_columns(first, last):
-    lane = lanes(first.shape[0])
-    own = jnp.where(lane < 8, first, 0.0)
-    return jnp.where((lane >= 56) & (lane < 64), pltpu.roll(last, 64, 1), own)
+            T[f][j, pl.ds(12, 8), :] = F[f][j, pl.ds(TOP, 8), :]
+            T[f][j, pl.ds(20, 8), :] = F[f][j, pl.ds(TOP + ROWS - 8, 8), :]
+        out = jnp.zeros((40, 128), jnp.float32)
+        for q in range(4):
+            at = pl.ds(TOP - 4 + 32 * q, 40)
+            in_east, east, in_west, west = edge_columns(F[f][0, at, :], F[f][3, at, :], q)
+            out = jnp.where(in_east, east, jnp.where(in_west, west, out))
+        G[f][0, pl.ds(8, 40), :] = out
 
 
 def unpack_lat(T, G, recv_s, recv_n):
-    behind, ahead = pl.ds(8, 8), pl.ds(32, 8)
-    for p in range(5):
-        f, g = 2 * p, 2 * p + 1
+    for f in range(9):
+        half = pl.ds(4 * (f % 2), 4)
         for j in range(4):
-            x = recv_s[p, j]
-            y = recv_n[p, j]
-            T[f][j, behind, :] = pltpu.roll(x, 4, 0)
-            T[f][j, ahead, :] = y
-            if g < 9:
-                T[g][j, behind, :] = x
-                T[g][j, ahead, :] = pltpu.roll(y, 4, 0)
-    for f in range(9):
-        G[f][0, pl.ds(TOP - 8, 8), :] = edge_columns(T[f][0, behind, :], T[f][3, behind, :])
-        G[f][0, pl.ds(TOP + ROWS, 8), :] = edge_columns(T[f][0, ahead, :], T[f][3, ahead, :])
+            T[f][j, pl.ds(8, 4), :] = recv_s[f // 2, j, half, :]
+            T[f][j, pl.ds(28, 4), :] = recv_n[f // 2, j, half, :]
+        for q, src, dst in ((0, pl.ds(8, 4), pl.ds(8, 4)), (3, pl.ds(28, 4), pl.ds(44, 4))):
+            in_east, east, in_west, west = edge_columns(T[f][0, src, :], T[f][3, src, :], q)
+            own = jnp.where(in_west, west, G[f][0, dst, :])
+            G[f][0, dst, :] = jnp.where(in_east, east, own)
 
 
 def unpack_lon(G, WE, WW):
-    n = 48
+    n = 40
     lane = lanes(n)
     ahead = lane % 8 < 4
-    halo = (lane >= 124) | ((lane >= 64) & (lane < 68))
-
-    def rows(i, carry):
-        src = pl.ds(pl.multiple_of(i * n + TOP - 8, 8), n)
-        x = jnp.where(ahead, pltpu.roll(WE[src, :], 64, 1), WW[src, :])
-        for f in range(9):
-            y = pltpu.roll(x, 128 - 8 * f, 1) if f else x
-            G[f][0, src, :] = jnp.where(halo, y, G[f][0, src, :])
-        return carry
-
-    lax.fori_loop(0, (ROWS + 16) // n, rows, 0)
+    x = []
+    for q in range(4):
+        at = pl.ds(TOP - 4 + 32 * q, n)
+        x.append(jnp.where(ahead, pltpu.roll(WE[at, :], 112, 1), WW[at, :]))
+    for f in range(9):
+        out = G[f][0, pl.ds(8, n), :]
+        for q in range(4):
+            in_east = (lane >= 32 * q + 8) & (lane < 32 * q + 12)
+            in_west = (lane >= 32 * q + 20) & (lane < 32 * q + 24)
+            out = jnp.where(in_east | in_west, turn(x[q], 32 * q + 24 - 8 * f), out)
+        G[f][0, pl.ds(8, n), :] = out
 
 
 def subcycle_rows(F, r, n):
@@ -208,28 +196,25 @@
 
 def subcycles_edges(T, G):
     def one(_, carry):
-        subcycle_rows(T, 8, 32)
-        for t in range(3):
-            subcycle_rows(G, TOP - 8 + 48 * t, 48)
+        subcycle_rows(T, 8, 24)
+        subcycle_rows(G, 8, 40)
         return carry
 
     lax.fori_loop(0, SUBCYCLES, one, 0)
 
 
 def merge_edges(F, T, G, fields):
-    low = sublanes() < 4
+    n = 32
+    lane = lanes(n)
     for f in fields:
         for j in range(4):
-            first, last = pl.ds(TOP, 8), pl.ds(TOP + ROWS - 8, 8)
-            F[f][j, first, :] = jnp.where(low, T[f][j, pl.ds(16, 8), :], F[f][j, first, :])
-            F[f][j, last, :] = jnp.where(low, F[f][j, last, :], T[f][j, pl.ds(24, 8), :])
-        n = 64
-        for i in range(ROWS // n):
-            at = pl.ds(TOP + i * n, n)
-            lane = lanes(n)
-            x = G[f][0, at, :]
-            F[f][0, at, :] = jnp.where(lane < 4, x, F[f][0, at, :])
-            F[f][3, at, :] = jnp.where(lane >= 124, pltpu.roll(x, 64, 1), F[f][3, at, :])
+            F[f][j, pl.ds(TOP, 4), :] = T[f][j, pl.ds(12, 4), :]
+            F[f][j, pl.ds(TOP + ROWS - 4, 4), :] = T[f][j, pl.ds(24, 4), :]
+        x = G[f][0, pl.ds(12, n), :]
+        for q in range(4):
+            at = pl.ds(TOP + n * q, n)
+            F[f][0, at, :] = jnp.where(lane < 4, turn(x, -32 * q - 24), F[f][0, at, :])
+            F[f][3, at, :] = jnp.where(lane >= 124, turn(x, 120 - 32 * q), F[f][3, at, :])
 
 
 def placing(own, place):
@@ -299,10 +284,14 @@
 
     has_e, has_w, has_n, has_s = gx < n_gx - 1, gx > 0, gy < n_gy - 1, gy > 0
 
-    every, inner, mid = pl.ds(0, ROWS), pl.ds(8, ROWS - 16), pl.ds(128, COLS - 256)
+    upper, lower = pl.ds(0, 64), pl.ds(64, 64)
+    inner, mid = pl.ds(8, ROWS - 16), pl.ds(128, COLS - 256)
+    left, right = pl.ds(0, 128), pl.ds(COLS - 128, 128)
     parts = (
-        (every, pl.ds(0, 128)),
-        (every, pl.ds(COLS - 128, 128)),
+        (upper, left),
+        (upper, right),
+        (lower, left),
+        (lower, right),
         (pl.ds(0, 8), mid),
         (pl.ds(ROWS - 8, 8), mid),
         (inner, mid),
@@ -322,14 +311,15 @@
         pltpu.make_async_copy(at, at, in_sem.at[k]).wait()
 
     masks = [
-        pltpu.make_async_copy(mask_ref.at[:, c], mask.at[:, c], in_sem.at[5 + k])
-        for k, c in enumerate((parts[0][1], parts[1][1], mid))
+        pltpu.make_async_copy(mask_ref.at[:, c], mask.at[:, c], in_sem.at[7 + k])
+        for k, c in enumerate((left, right, mid))
     ]
-    own_load = pltpu.make_async_copy(own_ref, own, in_sem.at[8])
+    own_load = pltpu.make_async_copy(own_ref, own, in_sem.at[10])
+    own_load.start()
+    masks[0].start()
+    masks[1].start()
     start_load(0)
-    masks[0].start()
     start_load(1)
-    masks[1].start()
 
     barrier = pltpu.get_barrier_semaphore()
     around = (
@@ -356,11 +346,12 @@
 
     start_load(2)
     start_load(3)
+    start_load(4)
+    start_load(5)
     masks[2].start()
-    start_load(4)
-    own_load.start()
-
-    for buf, tiles, ends in ((F, 4, (8, 144)), (T, 4, (0, 40)), (G, 1, (0, 152))):
+    start_load(6)
+
+    for buf, tiles, ends in ((F, 4, (8, 144)), (T, 4, (0, 32)), (G, 1, (0, 48))):
         for f in buf:
             for j in range(tiles):
                 for r in ends:
@@ -407,30 +398,32 @@
         def _():
             halo(k).start()
 
-    wait_load(0)
+    own_load.wait()
+    placing(own, place)
+
     masks[0].wait()
-    wait_load(1)
     masks[1].wait()
-    prepare((held, mask), F, 0, 2, 64, 64, (0, 3))
-    pack_lon(F, W)
+    for half in range(2):
+        wait_load(2 * half)
+        wait_load(2 * half + 1)
+        prepare((held, mask), F, 64 * half, 1, 0, 64, (0, 3))
+        pack_lon(F, W, 64 * half, 64)
     pl.semaphore_wait(barrier, greeted)
     for k in range(2, 8):
         start_halo(k)
 
-    wait_load(2)
-    wait_load(3)
+    wait_load(4)
+    wait_load(5)
     masks[2].wait()
     prepare((held, mask), F, 0, 2, ROWS - 8, 8, (1, 2))
     pack_lat(F, send_n, send_s)
     for k in (0, 1):
         start_halo(k)
 
-    wait_load(4)
+    wait_load(6)
     prepare((held, mask), F, 8, 2, 56, 56, (1, 2))
     copy_edges(F, T, G)
     subcycles_inside(F)
-    own_load.wait()
-    placing(own, place)
 
     for k in range(8):
 
@@ -445,19 +438,20 @@
     flatten_blocks(F, blocks)
     gather_blocks(place, blocks, send)
 
-    z, x = gy // 4, lax.rem(gy, 4)
     mine = pl.ds(pl.multiple_of(gy * 16, 16), 16)
-    for dz, dx in PEERS:
-        to = lax.rem(z + dz, 4) * 4 + lax.rem(x + dx, 4)
-        copy = pltpu.make_async_remote_copy(
-            src_ref=send.at[:, pl.ds(pl.multiple_of(to * 16, 16), 16), :],
-            dst_ref=vel_out.at[:, mine, :],
-            send_sem=out_sem.at[0],
-            recv_sem=out_sem.at[1],
-            device_id=(gx, to),
-            device_id_type=MESH,
-        )
-        copy.start()
+    for to in OWNERS:
+
+        @pl.when(gy != to)
+        def _(to=to):
+            pltpu.make_async_remote_copy(
+                src_ref=send.at[:, pl.ds(pl.multiple_of(to * 16, 16), 16), :],
+                dst_ref=vel_out.at[:, mine, :],
+                send_sem=out_sem.at[0],
+                recv_sem=out_sem.at[1],
+                device_id=(gx, to),
+                device_id_type=MESH,
+            ).start()
+
     local = pltpu.make_async_copy(send.at[:, mine, :], vel_out.at[:, mine, :], out_sem.at[2])
     local.start()
 
@@ -504,12 +498,12 @@
     args = [pltpu.with_memory_space_constraint(a, pltpu.HBM) for a in args]
     stress_shape, vel_shape = (3, ROWS, COLS), (2, 256, 256)
     scratch = [vmem((19, ROWS, COLS), f32)] + [vmem(a.shape, a.dtype) for a in args[6:]]
-    scratch += [vmem((4, HIGH, 128), f32)] * 9 + [vmem((4, 48, 128), f32)] * 9
-    scratch += [vmem((1, HIGH, 128), f32)] * 9
+    scratch += [vmem((4, HIGH, 128), f32)] * 9 + [vmem((4, 40, 128), f32)] * 9
+    scratch += [vmem((1, 56, 128), f32)] * 9
     scratch += [vmem((ROWS, 128), f32), vmem((HIGH, 128), f32), vmem((HIGH, 128), f32)]
     scratch += [vmem((5, 4, 8, 128), f32)] * 4
     scratch += [vmem((256, 256), jnp.bfloat16), vmem((256, 512), f32), vmem(vel_shape, f32)]
-    scratch += [dma((9,)), dma((8,)), dma((8,)), dma((3,))]
+    scratch += [dma((11,)), dma((8,)), dma((8,)), dma((3,))]
     held_stress, held_vel = pl.pallas_call(
         dynamics,
         out_shape=(vmem(stress_shape, f32), vmem(vel_shape, f32)),

time: 24.1 us -> 23.4 us (0.971)
  Pallas kernels: 23.4 us -> 22.6 us
    pallas_call x1, Pallas kernels: 22.3 us -> 21.5 us  [per_device(): pl.pallas_call(dynamics, out_shape=(vmem(stress_shape, f32), vmem(vel_sha...]
where the time goes in v4:
time: 23.4 us; the launch traced here: 23.2 us
  Pallas kernels  22.6 us (97%)
  between operations  0.64 us (3%)
    pallas_call x1, Pallas kernels, per_device(): pl.pallas_call(dynamics, out_shape=(vmem(stress_shape, f32), vmem(vel_sha...  21.5 us
    pallas_call x1, Pallas kernels, per_device(): pl.pallas_call(write_out, out_shape=(jax.ShapeDtypeStruct(stress_shape, f...  1.07 us

profile of v4, /device:TPU:1, one launch (start us, length us, event | category | flops | bytes accessed | tf_op | source)
XLA Modules:
  0.0 23.2 jit_solution(7173045246221831317)
XLA Ops:
  0.6 21.5 %shard_map.95 = (f32[3,128,512]{2,1,0:T(8,128)S(1)}, f32[2,256,256]{2,1,0:T(8,128)S(1)}) custom-call(f32[5,128,512]{2,1,0:T(8,128)} %vol_ref.1, f32[5,128,512]{2,1,0:T(8,128)} %area_ref.1, f32[2,128,512]{2,1,0:T(8,128)} %vel_ref.1, f32[2,128,512]{2,1,0:T(8,128)} %forc_ref.1, f32[2,128,512]{2,1,0:T(8,128)} %cur_ref.1, f32[3,128,512]{2,1,0:T(8,128)} %strs_ref.1, ...), custom_call_target="tpu_custom_call" | custom-call | tf_op jit(solution)/shard_map/pallas_call | solution.py:507
  22.2 1.1 %shard_map.96 = (f32[3,128,512]{2,1,0:T(8,128)}, f32[2,256,256]{2,1,0:T(8,128)}) custom-call(f32[3,128,512]{2,1,0:T(8,128)S(1)} %get-tuple-element.6.stress, f32[2,256,256]{2,1,0:T(8,128)S(1)} %get-tuple-element.7.vel), custom_call_target="tpu_custom_call" | custom-call | tf_op jit(solution)/shard_map/pallas_call | solution.py:519

commit v5 on v4

--- a/solution.py
+++ b/solution.py
@@ -200,7 +200,7 @@
         subcycle_rows(G, 8, 40)
         return carry
 
-    lax.fori_loop(0, SUBCYCLES, one, 0)
+    lax.fori_loop(0, SUBCYCLES, one, 0, unroll=True)
 
 
 def merge_edges(F, T, G, fields):

time: 23.4 us -> 23.1 us (0.987)
    pallas_call x1, Pallas kernels: 21.5 us -> 21.3 us  [per_device(): pl.pallas_call(dynamics, out_shape=(vmem(stress_shape, f32), vmem(vel_sha...]
where the time goes in v5:
time: 23.1 us; the launch traced here: 23 us
  Pallas kernels  22.4 us (97%)
  between operations  0.64 us (3%)
    pallas_call x1, Pallas kernels, per_device(): pl.pallas_call(dynamics, out_shape=(vmem(stress_shape, f32), vmem(vel_sha...  21.3 us
    pallas_call x1, Pallas kernels, per_device(): pl.pallas_call(write_out, out_shape=(jax.ShapeDtypeStruct(stress_shape, f...  1.07 us

profile of v5, /device:TPU:1, one launch (start us, length us, event | category | flops | bytes accessed | tf_op | source)
XLA Modules:
  0.0 23.0 jit_solution(5620298226098015301)
XLA Ops:
  0.6 21.3 %shard_map.95 = (f32[3,128,512]{2,1,0:T(8,128)S(1)}, f32[2,256,256]{2,1,0:T(8,128)S(1)}) custom-call(f32[5,128,512]{2,1,0:T(8,128)} %vol_ref.1, f32[5,128,512]{2,1,0:T(8,128)} %area_ref.1, f32[2,128,512]{2,1,0:T(8,128)} %vel_ref.1, f32[2,128,512]{2,1,0:T(8,128)} %forc_ref.1, f32[2,128,512]{2,1,0:T(8,128)} %cur_ref.1, f32[3,128,512]{2,1,0:T(8,128)} %strs_ref.1, ...), custom_call_target="tpu_custom_call" | custom-call | tf_op jit(solution)/shard_map/pallas_call | solution.py:507
  21.9 1.1 %shard_map.96 = (f32[3,128,512]{2,1,0:T(8,128)}, f32[2,256,256]{2,1,0:T(8,128)}) custom-call(f32[3,128,512]{2,1,0:T(8,128)S(1)} %get-tuple-element.6.stress, f32[2,256,256]{2,1,0:T(8,128)S(1)} %get-tuple-element.7.vel), custom_call_target="tpu_custom_call" | custom-call | tf_op jit(solution)/shard_map/pallas_call | solution.py:519
